TPU v7x, 256 devices: a whole 4x4x8 slice. The times are simulated.
256 devices in a mesh: board: 64 (over z, x_hi, y), river: 2 (over core), hand: 2 (over x_lo).
Axes of the slice: x: 4 (x_hi: 2, x_lo: 2; x = x_hi * 2 + x_lo), y: 4, z: 8, core: 2. Of those that a mesh axis runs over, the one named last changes fastest.
Arguments:
- reach_probs: float32 [256, 2, 1326], P('board', None, 'hand'), may hold values from 0 to 1
- turn_cards: int32 [256, 4], P('board'), may hold values from 0 to 51, as said below
- river_cards: int32 [256, 48], P('board', 'river'), may hold values from 0 to 51, as said below
- hand_ranks: int32 [256, 48, 1326], P('board', 'river'), may hold values from 0 to 1325
- pot_chips: int32 [256], P('board'), may hold values from 100 to 399
- bet_chips: int32 [256, 2], P('board'), may hold values from 10 to 299
- regrets_first: float32 [256, 48, 3, 1326], P('board', 'river', None, 'hand'), may hold values from 0.01 to 1
- regrets_second: float32 [256, 48, 4, 1326], P('board', 'river', None, 'hand'), may hold values from 0.01 to 1
Outputs:
- turn_values: float32 [256, 2, 1326], P('board', None, 'hand')
- flop_values: float32 [2, 1326], P(None, 'hand')
- new_regrets_first: float32 [256, 48, 3, 1326], P('board', 'river', None, 'hand')
- new_regrets_second: float32 [256, 48, 4, 1326], P('board', 'river', None, 'hand')
Inputs may be any that keep to these rules, and one draw needn't show every extreme that they name: For each turn board, the four turn_cards and the 48 river_cards together name every card of the deck once. `river_cards`: see turn_cards.
All inputs are finite; a program needn't handle non-finite values.
Results may differ from a plain program's by a relative error of at most 0.0003.
Values may be sent and summed in bfloat16 or wider, within the bound.
No kernel may reach another device: no remote copies, remote signals or barrier semaphores. Data moves between devices by JAX's collectives and lax.ppermute only.
A program may use at most 64 MiB of HBM per device.

v0:
```python
import jax
import jax.numpy as jnp
import numpy as np
from jax import lax
from jax.sharding import PartitionSpec as P

DECK = 52
HANDS = 1326
RIVERS = 48


def incidence_table():
    lower_card, upper_card = np.triu_indices(DECK, 1)
    card_ids = np.arange(DECK)
    hand_table = (card_ids[None, :] == lower_card[:, None]) | (
        card_ids[None, :] == upper_card[:, None]
    )
    return jnp.asarray(hand_table.astype(np.float32)).astype(jnp.bfloat16)


def pair_block():
    for candidate in (8, 6, 4, 3, 2, 1):
        return candidate
    return 1


def signed_table(first_ranks, second_ranks, compat):
    signs = jnp.where(
        first_ranks[:, :, None] > second_ranks[:, None, :],
        1.0,
        jnp.where(first_ranks[:, :, None] < second_ranks[:, None, :], -1.0, 0.0),
    )
    return signs.astype(jnp.bfloat16) * compat[None]


def settle(
    showdown,
    contact_sums,
    strategy,
    call_prob,
    alive_mask,
    regrets_first,
    regrets_second,
    small_share,
    large_share,
):
    oop_check = 0.5 * showdown[..., 0, :]
    oop_small = (
        0.5 * (contact_sums[..., 0, :] - contact_sums[..., 1, :])
        + (0.5 + small_share) * showdown[..., 1, :]
    )
    oop_large = (
        0.5 * (contact_sums[..., 0, :] - contact_sums[..., 2, :])
        + (0.5 + large_share) * showdown[..., 2, :]
    )
    action_values = jnp.stack([oop_check, oop_small, oop_large], axis=-2) * alive_mask[..., None, :]
    oop_values = jnp.sum(strategy * action_values, axis=-2)
    new_first = jnp.maximum(regrets_first + action_values - oop_values[..., None, :], 0.0)
    fold_small = -0.5 * contact_sums[..., 4, :] * alive_mask
    call_small = (0.5 + small_share) * showdown[..., 4, :] * alive_mask
    fold_large = -0.5 * contact_sums[..., 5, :] * alive_mask
    call_large = (0.5 + large_share) * showdown[..., 5, :] * alive_mask
    node_small = (1.0 - call_prob[..., 0, :]) * fold_small + call_prob[..., 0, :] * call_small
    node_large = (1.0 - call_prob[..., 1, :]) * fold_large + call_prob[..., 1, :] * call_large
    ip_values = 0.5 * showdown[..., 3, :] * alive_mask + node_small + node_large
    utility = jnp.stack([fold_small, call_small, fold_large, call_large], axis=-2)
    node_values = jnp.stack([node_small, node_small, node_large, node_large], axis=-2)
    new_second = jnp.maximum(regrets_second + utility - node_values, 0.0)
    return (oop_values, ip_values, new_first, new_second)


def shards(
    reach_probs,
    turn_cards,
    river_cards,
    hand_ranks,
    pot_chips,
    bet_chips,
    regrets_first,
    regrets_second,
):
    turns_here, rivers_here = river_cards.shape
    hands_here = reach_probs.shape[2]
    pair_count = turns_here * rivers_here
    block_pairs_count = pair_block()
    block_total = pair_count // block_pairs_count
    contract = (((1,), (1,)), ((), ()))
    batched = (((2,), (2,)), ((0,), (0,)))
    incidence = incidence_table()
    hand_offset = lax.axis_index("hand") * hands_here
    own_incidence = lax.dynamic_slice_in_dim(incidence, hand_offset, hands_here, 0)
    deck_ids = jnp.arange(DECK, dtype=jnp.int32)
    dead_turn = jnp.any(turn_cards[:, :, None] == deck_ids[None, None, :], axis=1)
    dead_cards = (
        dead_turn[:, None, :] | (river_cards[:, :, None] == deck_ids[None, None, :])
    ).astype(jnp.bfloat16)
    alive_mask = (
        jnp.dot(
            dead_cards.reshape(pair_count, DECK),
            own_incidence.T,
            preferred_element_type=jnp.float32,
        )
        == 0
    )
    alive_mask = alive_mask.astype(jnp.float32).reshape(turns_here, rivers_here, hands_here)
    scaling = 2.0 / HANDS
    oop_reach = reach_probs[:, 0][:, None, :] * scaling * alive_mask
    ip_reach = reach_probs[:, 1][:, None, :] * scaling * alive_mask
    strategy = regrets_first / jnp.sum(regrets_first, axis=2, keepdims=True)
    call_prob = regrets_second[:, :, 1::2] / (
        regrets_second[:, :, 0::2] + regrets_second[:, :, 1::2]
    )
    operand_rows = jnp.stack(
        [
            ip_reach,
            ip_reach * call_prob[:, :, 0],
            ip_reach * call_prob[:, :, 1],
            oop_reach * strategy[:, :, 0],
            oop_reach * strategy[:, :, 1],
            oop_reach * strategy[:, :, 2],
        ],
        axis=2,
    ).astype(jnp.bfloat16)
    operand_flat = operand_rows.reshape(pair_count * 6, hands_here)
    rank_flat = hand_ranks.reshape(pair_count, HANDS)
    own_ranks = lax.dynamic_slice_in_dim(rank_flat, hand_offset, hands_here, 1)
    own_blocks = own_ranks.reshape(block_total, block_pairs_count, hands_here)
    starting = (
        jnp.zeros((pair_count, 6, hands_here), jnp.float32),
        jnp.zeros((pair_count * 6, hands_here), jnp.float32),
    )
    block_rows = lax.all_gather(operand_flat, "hand", axis=1, tiled=True)
    width = block_rows.shape[1]
    other_incidence = lax.slice_in_dim(incidence, 0, width, axis=0)
    intersection = jnp.dot(own_incidence, other_incidence.T, preferred_element_type=jnp.float32)
    compat = (intersection == 0).astype(jnp.bfloat16)
    contact_part = lax.dot_general(block_rows, compat, contract, preferred_element_type=jnp.float32)
    other_blocks = rank_flat.reshape(block_total, block_pairs_count, width)
    row_blocks = block_rows.reshape(block_total, block_pairs_count, 6, width)

    def per_block(items):
        mine_rank, their_rank, rows_six = items
        signed = signed_table(mine_rank, their_rank, compat)
        return lax.dot_general(rows_six, signed, batched, preferred_element_type=jnp.float32)

    showdown_part = lax.map(per_block, (own_blocks, other_blocks, row_blocks))
    showdown_part = showdown_part.reshape(pair_count, 6, hands_here)
    showdown_flat = starting[0] + showdown_part
    contact_flat = starting[1] + contact_part
    showdown = showdown_flat.reshape(turns_here, rivers_here, 6, hands_here)
    contact_sums = contact_flat.reshape(turns_here, rivers_here, 6, hands_here)
    bet_share = bet_chips.astype(jnp.float32) / pot_chips.astype(jnp.float32)[:, None]
    small_share = bet_share[:, 0][:, None, None]
    large_share = bet_share[:, 1][:, None, None]
    oop_values, ip_values, new_first, new_second = settle(
        showdown,
        contact_sums,
        strategy,
        call_prob,
        alive_mask,
        regrets_first,
        regrets_second,
        small_share,
        large_share,
    )
    turn_partial = jnp.stack([jnp.sum(oop_values, axis=1), jnp.sum(ip_values, axis=1)], axis=1)
    turn_values = lax.psum(turn_partial, "river") / RIVERS
    flop_values = lax.psum(jnp.sum(turn_values, axis=0), "board")
    return (turn_values, flop_values, new_first, new_second)


def solution(mesh):
    placed = (
        P("board", None, "hand"),
        P("board", None),
        P("board", "river"),
        P("board", "river", None),
        P("board"),
        P("board", None),
        P("board", "river", None, "hand"),
        P("board", "river", None, "hand"),
    )
    return jax.shard_map(
        shards,
        mesh=mesh,
        in_specs=placed,
        out_specs=(
            P("board", None, "hand"),
            P(None, "hand"),
            P("board", "river", None, "hand"),
            P("board", "river", None, "hand"),
        ),
        check_vma=False,
    )
```

profile of v0, /device:TPU:2, one launch (start us, length us, event | category | flops | bytes accessed | tf_op | source)
XLA Modules:
  0.0 412.2 jit_solution(10839442515214869509)
XLA Ops:
  7.3 9.3 %slice.73 = f32[4,24,2,663]{3,2,1,0:T(2,128)S(1)} slice(f32[4,24,4,663]{3,2,1,0:T(4,128)} %param.18), slice={[0:4:1], [0:24:1], [1:4:2], [0:663:1]} | slice | bytes 1018368 | tf_op jit(solution)/shard_map/slice | solution.py:110
  16.6 9.3 %slice.74 = f32[4,24,2,663]{3,2,1,0:T(2,128)S(1)} slice(f32[4,24,4,663]{3,2,1,0:T(4,128)} %param.18), slice={[0:4:1], [0:24:1], [0:4:2], [0:663:1]} | slice | bytes 1018368 | tf_op jit(solution)/shard_map/slice | solution.py:111
  37.2 2.4 fusion.62
  39.6 32.3 %all-gather.3.cloned.1.call-done = bf16[2,663,576]{2,1,0:T(8,128)(2,1)} async-done(((bf16[1,663,576]{2,1,0:T(8,128)(2,1)}), bf16[2,663,576]{2,1,0:T(8,128)(2,1)}) %all-gather.3.cloned.1.call-update) | async-done | bytes 1527568 | tf_op jit(solution)/shard_map/all_gather | solution.py:132
  74.1 2.3 copy.131
  76.4 3.9 reshape.97
  80.3 113.9 %while.10 = (s32[]{:T(128)}, f32[12,8,6,663]{3,1,0,2:T(8,128)}, bf16[12,8,6,1326]{3,2,1,0:T(8,128)(2,1)}, s32[12,8,663]{2,1,0:T(8,128)}, s32[12,8,1326]{2,1,0:T(8,128)}, /*index=5*/bf16[663,1326]{1,0:T(8,128)(2,1)}, s32[]{:T(128)}) while((s32[]{:T(128)}, f32[12,8,6,663]{3,1,0,2:T(8,128)}, bf16[12,8,6,1326]{3,2,1,0:T(8,128)(2,1)}, ...), condition=%wide.region_3.4_spmd, body=%wide.region_2.3_spmd.sunk | while | flops 126595872 | bytes 2644149 | solution.py:146
  81.8 7.2 %fusion.72 = f32[1,8,6,663]{3,2,1,0:T(8,128)S(1)} fusion(s32[8,1326]{1,0:T(8,128)S(1)} %dynamic-slice_bitcast_fusion.5, s32[8,663]{1,0:T(8,128)S(1)} %dynamic-slice_bitcast_fusion.6, bf16[663,1326]{1,0:T(8,128)(2,1)} %get-tuple-element.154, bf16[12,8,6,1326]{3,2,1,0:T(8,128)(2,1)} %get-tuple-element.151, s32[]{:T(128)} %get-tuple-element.142), kind=kOutput, calls=%fused_computation.4.clone.1 | convolution fusion | flops 126595872 | bytes 2241504 | tf_op jit(solution)/shard_map/while/body/eval_jaxpr/dot_general | solution.py:144
  91.4 7.2 %fusion.72 = f32[1,8,6,663]{3,2,1,0:T(8,128)S(1)} fusion(s32[8,1326]{1,0:T(8,128)S(1)} %dynamic-slice_bitcast_fusion.5, s32[8,663]{1,0:T(8,128)S(1)} %dynamic-slice_bitcast_fusion.6, bf16[663,1326]{1,0:T(8,128)(2,1)} %get-tuple-element.154, bf16[12,8,6,1326]{3,2,1,0:T(8,128)(2,1)} %get-tuple-element.151, s32[]{:T(128)} %get-tuple-element.142), kind=kOutput, calls=%fused_computation.4.clone.1 | convolution fusion | flops 126595872 | bytes 2241504 | tf_op jit(solution)/shard_map/while/body/eval_jaxpr/dot_general | solution.py:144
  100.8 7.2 %fusion.72 = f32[1,8,6,663]{3,2,1,0:T(8,128)S(1)} fusion(s32[8,1326]{1,0:T(8,128)S(1)} %dynamic-slice_bitcast_fusion.5, s32[8,663]{1,0:T(8,128)S(1)} %dynamic-slice_bitcast_fusion.6, bf16[663,1326]{1,0:T(8,128)(2,1)} %get-tuple-element.154, bf16[12,8,6,1326]{3,2,1,0:T(8,128)(2,1)} %get-tuple-element.151, s32[]{:T(128)} %get-tuple-element.142), kind=kOutput, calls=%fused_computation.4.clone.1 | convolution fusion | flops 126595872 | bytes 2241504 | tf_op jit(solution)/shard_map/while/body/eval_jaxpr/dot_general | solution.py:144
  110.3 7.2 %fusion.72 = f32[1,8,6,663]{3,2,1,0:T(8,128)S(1)} fusion(s32[8,1326]{1,0:T(8,128)S(1)} %dynamic-slice_bitcast_fusion.5, s32[8,663]{1,0:T(8,128)S(1)} %dynamic-slice_bitcast_fusion.6, bf16[663,1326]{1,0:T(8,128)(2,1)} %get-tuple-element.154, bf16[12,8,6,1326]{3,2,1,0:T(8,128)(2,1)} %get-tuple-element.151, s32[]{:T(128)} %get-tuple-element.142), kind=kOutput, calls=%fused_computation.4.clone.1 | convolution fusion | flops 126595872 | bytes 2241504 | tf_op jit(solution)/shard_map/while/body/eval_jaxpr/dot_general | solution.py:144
  119.8 7.2 %fusion.72 = f32[1,8,6,663]{3,2,1,0:T(8,128)S(1)} fusion(s32[8,1326]{1,0:T(8,128)S(1)} %dynamic-slice_bitcast_fusion.5, s32[8,663]{1,0:T(8,128)S(1)} %dynamic-slice_bitcast_fusion.6, bf16[663,1326]{1,0:T(8,128)(2,1)} %get-tuple-element.154, bf16[12,8,6,1326]{3,2,1,0:T(8,128)(2,1)} %get-tuple-element.151, s32[]{:T(128)} %get-tuple-element.142), kind=kOutput, calls=%fused_computation.4.clone.1 | convolution fusion | flops 126595872 | bytes 2241504 | tf_op jit(solution)/shard_map/while/body/eval_jaxpr/dot_general | solution.py:144
  129.3 7.2 %fusion.72 = f32[1,8,6,663]{3,2,1,0:T(8,128)S(1)} fusion(s32[8,1326]{1,0:T(8,128)S(1)} %dynamic-slice_bitcast_fusion.5, s32[8,663]{1,0:T(8,128)S(1)} %dynamic-slice_bitcast_fusion.6, bf16[663,1326]{1,0:T(8,128)(2,1)} %get-tuple-element.154, bf16[12,8,6,1326]{3,2,1,0:T(8,128)(2,1)} %get-tuple-element.151, s32[]{:T(128)} %get-tuple-element.142), kind=kOutput, calls=%fused_computation.4.clone.1 | convolution fusion | flops 126595872 | bytes 2241504 | tf_op jit(solution)/shard_map/while/body/eval_jaxpr/dot_general | solution.py:144
  138.8 7.2 %fusion.72 = f32[1,8,6,663]{3,2,1,0:T(8,128)S(1)} fusion(s32[8,1326]{1,0:T(8,128)S(1)} %dynamic-slice_bitcast_fusion.5, s32[8,663]{1,0:T(8,128)S(1)} %dynamic-slice_bitcast_fusion.6, bf16[663,1326]{1,0:T(8,128)(2,1)} %get-tuple-element.154, bf16[12,8,6,1326]{3,2,1,0:T(8,128)(2,1)} %get-tuple-element.151, s32[]{:T(128)} %get-tuple-element.142), kind=kOutput, calls=%fused_computation.4.clone.1 | convolution fusion | flops 126595872 | bytes 2241504 | tf_op jit(solution)/shard_map/while/body/eval_jaxpr/dot_general | solution.py:144
  148.3 7.2 %fusion.72 = f32[1,8,6,663]{3,2,1,0:T(8,128)S(1)} fusion(s32[8,1326]{1,0:T(8,128)S(1)} %dynamic-slice_bitcast_fusion.5, s32[8,663]{1,0:T(8,128)S(1)} %dynamic-slice_bitcast_fusion.6, bf16[663,1326]{1,0:T(8,128)(2,1)} %get-tuple-element.154, bf16[12,8,6,1326]{3,2,1,0:T(8,128)(2,1)} %get-tuple-element.151, s32[]{:T(128)} %get-tuple-element.142), kind=kOutput, calls=%fused_computation.4.clone.1 | convolution fusion | flops 126595872 | bytes 2241504 | tf_op jit(solution)/shard_map/while/body/eval_jaxpr/dot_general | solution.py:144
  157.8 7.2 %fusion.72 = f32[1,8,6,663]{3,2,1,0:T(8,128)S(1)} fusion(s32[8,1326]{1,0:T(8,128)S(1)} %dynamic-slice_bitcast_fusion.5, s32[8,663]{1,0:T(8,128)S(1)} %dynamic-slice_bitcast_fusion.6, bf16[663,1326]{1,0:T(8,128)(2,1)} %get-tuple-element.154, bf16[12,8,6,1326]{3,2,1,0:T(8,128)(2,1)} %get-tuple-element.151, s32[]{:T(128)} %get-tuple-element.142), kind=kOutput, calls=%fused_computation.4.clone.1 | convolution fusion | flops 126595872 | bytes 2241504 | tf_op jit(solution)/shard_map/while/body/eval_jaxpr/dot_general | solution.py:144
  167.3 7.2 %fusion.72 = f32[1,8,6,663]{3,2,1,0:T(8,128)S(1)} fusion(s32[8,1326]{1,0:T(8,128)S(1)} %dynamic-slice_bitcast_fusion.5, s32[8,663]{1,0:T(8,128)S(1)} %dynamic-slice_bitcast_fusion.6, bf16[663,1326]{1,0:T(8,128)(2,1)} %get-tuple-element.154, bf16[12,8,6,1326]{3,2,1,0:T(8,128)(2,1)} %get-tuple-element.151, s32[]{:T(128)} %get-tuple-element.142), kind=kOutput, calls=%fused_computation.4.clone.1 | convolution fusion | flops 126595872 | bytes 2241504 | tf_op jit(solution)/shard_map/while/body/eval_jaxpr/dot_general | solution.py:144
  176.8 7.2 %fusion.72 = f32[1,8,6,663]{3,2,1,0:T(8,128)S(1)} fusion(s32[8,1326]{1,0:T(8,128)S(1)} %dynamic-slice_bitcast_fusion.5, s32[8,663]{1,0:T(8,128)S(1)} %dynamic-slice_bitcast_fusion.6, bf16[663,1326]{1,0:T(8,128)(2,1)} %get-tuple-element.154, bf16[12,8,6,1326]{3,2,1,0:T(8,128)(2,1)} %get-tuple-element.151, s32[]{:T(128)} %get-tuple-element.142), kind=kOutput, calls=%fused_computation.4.clone.1 | convolution fusion | flops 126595872 | bytes 2241504 | tf_op jit(solution)/shard_map/while/body/eval_jaxpr/dot_general | solution.py:144
  186.3 7.2 %fusion.72 = f32[1,8,6,663]{3,2,1,0:T(8,128)S(1)} fusion(s32[8,1326]{1,0:T(8,128)S(1)} %dynamic-slice_bitcast_fusion.5, s32[8,663]{1,0:T(8,128)S(1)} %dynamic-slice_bitcast_fusion.6, bf16[663,1326]{1,0:T(8,128)(2,1)} %get-tuple-element.154, bf16[12,8,6,1326]{3,2,1,0:T(8,128)(2,1)} %get-tuple-element.151, s32[]{:T(128)} %get-tuple-element.142), kind=kOutput, calls=%fused_computation.4.clone.1 | convolution fusion | flops 126595872 | bytes 2241504 | tf_op jit(solution)/shard_map/while/body/eval_jaxpr/dot_general | solution.py:144
  194.3 4.2 %fusion.63 = f32[576,663]{1,0:T(8,128)} fusion(bf16[1326,576]{1,0:T(8,128)(2,1)S(1)} %reshape.102, pred[663,1326]{1,0:T(8,128)(4,1)} %get-tuple-element.95), kind=kOutput, calls=%fused_computation.107 | convolution fusion | flops 1012766976 | bytes 3934242 | tf_op jit(solution)/shard_map/dot_general | solution.py:137
  198.5 2.7 reshape.100
  201.2 6.2 %fusion.61 = (f32[4,24,1,663]{3,2,1,0:T(1,128)S(1)}, f32[4,24,1,663]{3,2,1,0:T(1,128)S(1)}, f32[4,24,1,663]{3,2,1,0:T(1,128)S(1)}, f32[4,24,1,663]{3,2,1,0:T(1,128)S(1)}, f32[4,24,1,663]{3,2,1,0:T(1,128)S(1)}) fusion(f32[4,24,6,663]{3,2,1,0:T(8,128)} %reshape.100), kind=kLoop, calls=%fused_computation.105 | loop fusion | bytes 2545920 | tf_op jit(solution)/shard_map/slice | solution.py:49
  214.7 3.4 psum.14
  218.8 186.5 %psum.15 = f32[2,663]{1,0:T(2,128)} all-reduce(f32[2,663]{1,0:T(2,128)S(1)} %get-tuple-element.88), channel_id=1, replica_groups=mesh['board'=64,'river'=2,'hand'=2] {'board'}, use_global_device_ids=true, to_apply=%region_8.9 | all-reduce | flops 1326 | bytes 10608 | tf_op jit(solution)/shard_map/psum | solution.py:168
  (95 shorter events, 48.4 us)
Async XLA Ops:
  7.2 19.0 %copy-start.5 = (bf16[1326,52]{1,0:T(8,128)(2,1)S(1)}, bf16[1326,52]{1,0:T(8,128)(2,1)}, u32[]{:S(2)}) copy-start(bf16[1326,52]{1,0:T(8,128)(2,1)} %constant.61) | copy-start | bytes 413716
  7.2 18.7 %copy-start.7 = (s32[4,4]{1,0:T(4,128)S(1)}, s32[4,4]{1,0:T(4,128)}, u32[]{:S(2)}) copy-start(s32[4,4]{1,0:T(4,128)} %param.12) | copy-start | bytes 196
  7.2 18.8 %copy-start.8 = (s32[4,24]{1,0:T(4,128)S(1)}, s32[4,24]{1,0:T(4,128)}, u32[]{:S(2)}) copy-start(s32[4,24]{1,0:T(4,128)} %param.13) | copy-start | bytes 1156
  7.2 18.9 %copy-start.6 = (f32[4,2,663]{2,1,0:T(2,128)S(1)}, f32[4,2,663]{2,1,0:T(2,128)}, u32[]{:S(2)}) copy-start(f32[4,2,663]{2,1,0:T(2,128)} %param.11) | copy-start | bytes 63652
  7.2 64.7 %all-gather.3.cloned.1.call-start = ((), (), s32[]{:S(2)}) async-start(), calls=%async_computation | async-start | bytes 2549760 | tf_op jit(solution)/shard_map/all_gather | solution.py:132
  26.4 2.2 copy-start
  28.7 1.5 copy-start.2
  34.0 2.3 copy-start.10
  34.0 2.3 copy-start.4
  34.0 3.2 copy-start.9
  207.4 1.5 copy-start.1
  212.0 1.3 copy-start.3
Sparse Core Ops, SparseCore 0:
  36.4 35.4 all-gather.2
where the time goes:
time: 415 us; the launch traced here: 412 us
  blocking collectives  190 us (46%)
  matrix products  93.7 us (23%)
  local copies, waits for them, and re-layouts  72.5 us (17%)
  waiting for transfers between devices  32.3 us (8%)
  between operations  14.3 us (3%)
  other arithmetic  9.36 us (2%)
    psum x1, blocking collectives, shards(): flop_values = lax.psum(jnp.sum(turn_values, axis=0), 'board')  187 us
    dot_general x12, matrix products, per_block(): lax.dot_general(rows_six, signed, batched, preferred_element_type=jnp.flo...  86.8 us
    all_gather x1, waiting for transfers between devices, shards(): block_rows = lax.all_gather(operand_flat, 'hand', axis=1, tiled=True)  32.3 us
    gt x24, local copies, waits for them, and re-layouts, signed_table(): first_ranks[:, :, None] > second_ranks[:, None, :]  18.4 us
    unnamed x29, local copies, waits for them, and re-layouts  9.95 us
    slice x1, local copies, waits for them, and re-layouts, shards(): regrets_second[:, :, 1::2]  9.33 us
    slice x1, local copies, waits for them, and re-layouts, shards(): regrets_second[:, :, 0::2] + regrets_second[:, :, 1::2]  9.29 us
    dynamic_update_slice x12, local copies, waits for them, and re-layouts, shards(): showdown_part = lax.map(per_block, (own_blocks, other_blocks, row_blocks))  8.71 us
  transfers between devices with their start and end apart: 1, of which 1 were waited for; matrix products, arithmetic and copies ran while one was open for 1% of the time, Pallas kernels for 0%

commit v1 on v0

v1 whole, which is shorter than its diff:
```python
import functools

import jax
import jax.numpy as jnp
import numpy as np
from jax import lax
from jax.experimental import pallas as pl
from jax.experimental.pallas import tpu as pltpu
from jax.sharding import Mesh
from jax.sharding import PartitionSpec as P

DECK = 52
HANDS = 1326
RIVERS = 48
HALF = HANDS // 2
TILES = 6
WIDTH = TILES * 128
DEPTH = 672
TURNS_HERE = 4
RIVERS_HERE = 24
PAIRS = TURNS_HERE * RIVERS_HERE
UNROLL = 4
VMEM_LIMIT = 56 << 20


def card_tables():
    lower, upper = np.triu_indices(DECK, 1)
    halves = np.full((2, 2, WIDTH), -1, np.int32)
    for half in range(2):
        halves[half, 0, :HALF] = lower[half * HALF : (half + 1) * HALF]
        halves[half, 1, :HALF] = upper[half * HALF : (half + 1) * HALF]
    compat = np.zeros((2, 2, WIDTH, WIDTH), np.float32)
    for own in range(2):
        for slot in range(2):
            other = own ^ slot
            shares = np.zeros((WIDTH, WIDTH), bool)
            for i in range(2):
                for j in range(2):
                    shares |= halves[other, i][:, None] == halves[own, j][None, :]
            compat[own, slot, :HALF, :HALF] = ~shares[:HALF, :HALF]
    return halves, compat


def alive_rows(cards_ref, turn_ref, river_ref, hand, turn):
    low = jnp.where(hand == 0, cards_ref[0, 0:1, :], cards_ref[1, 0:1, :])
    high = jnp.where(hand == 0, cards_ref[0, 1:2, :], cards_ref[1, 1:2, :])
    good = low >= 0
    for k in range(4):
        dead = turn_ref[turn, k]
        good = good & (low != dead) & (high != dead)
    row = jnp.broadcast_to(river_ref[turn : turn + 1, :], (RIVERS_HERE, RIVERS_HERE))
    diagonal = lax.broadcasted_iota(jnp.int32, row.shape, 0) == lax.broadcasted_iota(
        jnp.int32, row.shape, 1
    )
    column = jnp.sum(jnp.where(diagonal, row, 0), axis=1, keepdims=True)
    column = jnp.broadcast_to(column, (RIVERS_HERE, 128))
    low = jnp.broadcast_to(low, column.shape)
    high = jnp.broadcast_to(high, column.shape)
    good = jnp.broadcast_to(good.astype(jnp.int32), column.shape)
    return (good > 0) & (low != column) & (high != column)


def second_rows(flat, turn, b):
    base = turn * RIVERS_HERE * 4 + 2 * b
    fold = flat[pl.ds(base, RIVERS_HERE, stride=4), :]
    call = flat[pl.ds(base + 1, RIVERS_HERE, stride=4), :]
    return fold, call


def operand_kernel(turn_ref, river_ref, cards_ref, reach_ref, first_ref, second_ref, out_ref):
    hand = lax.axis_index("hand")
    flat = second_ref.reshape(PAIRS * 4, 128)
    scaling = 2.0 / HANDS
    for two in range(TURNS_HERE // 2):
        parts = []
        for turn in (2 * two, 2 * two + 1):
            alive = alive_rows(cards_ref, turn_ref, river_ref, hand, turn)
            x = jnp.where(alive, reach_ref[turn, 0:1, :] * scaling, 0.0)
            y = jnp.where(alive, reach_ref[turn, 1:2, :] * scaling, 0.0)
            actions = [first_ref[turn, a] for a in range(3)]
            total = actions[0] + actions[1] + actions[2]
            rows = [y]
            for b in range(2):
                fold, call = second_rows(flat, turn, b)
                rows.append(jnp.where(alive, y * (call / (fold + call)), 0.0))
            for a in range(3):
                rows.append(jnp.where(alive, x * (actions[a] / total), 0.0))
            parts.append(rows)
        for c in range(6):
            both = jnp.concatenate([parts[0][c], parts[1][c]], axis=0)
            start = c * PAIRS + two * 2 * RIVERS_HERE
            out_ref[0, start : start + 2 * RIVERS_HERE, :] = both.astype(jnp.bfloat16)


def ordered(ranks):
    return lax.shift_left((ranks & 127) + 128, lax.shift_right_logical(ranks, 7)).astype(
        jnp.float32
    )


def sums_kernel(
    slot,
    ranks_ref,
    ops_ref,
    table_ref,
    *refs,
):
    if slot == 0:
        start_refs = None
        show_ref, contact_ref = refs[:2]
        refs = refs[2:]
    else:
        start_refs = refs[:2]
        show_ref, contact_ref = refs[2:4]
        refs = refs[4:]
    compat, negative, rows, staged, columns, rolled, wide, sem = refs
    hand = lax.axis_index("hand")
    fetch = pltpu.make_async_copy(table_ref.at[hand, slot], compat, sem)
    fetch.start()

    lower = ordered(ranks_ref[:, :HALF])
    upper = ordered(ranks_ref[:, HALF:])
    rows[...] = jnp.zeros_like(rows)
    staged[...] = jnp.zeros_like(staged)
    rows[:, :HALF] = jnp.where(hand == 0, lower, upper)
    staged[:PAIRS, :HALF] = jnp.where(hand == slot, lower, upper)
    for tile in range(TILES):
        columns[tile * 128 : (tile + 1) * 128, :] = staged[:, tile * 128 : (tile + 1) * 128].T
        wide[tile, : 6 * PAIRS, :] = ops_ref[tile].astype(jnp.float32)
        wide[tile, 6 * PAIRS :, :] = jnp.zeros((2 * PAIRS, 128), jnp.float32)
    fetch.wait()
    negative[...] = -compat[...]

    chunk = 2 * PAIRS
    for m in range(3):
        for n in range(3):
            acc = jnp.zeros((chunk, 256), jnp.float32)
            for k in range(3):
                left = jnp.concatenate(
                    [ops_ref[2 * k + i, m * chunk : (m + 1) * chunk, :] for i in range(2)], axis=1
                )
                acc += jnp.dot(
                    left,
                    compat[k * 256 : (k + 1) * 256, n * 256 : (n + 1) * 256],
                    preferred_element_type=jnp.float32,
                )
            for i in range(2):
                value = acc[:, i * 128 : (i + 1) * 128]
                if start_refs is not None:
                    value = value + start_refs[1][2 * n + i, m * chunk : (m + 1) * chunk, :]
                contact_ref[2 * n + i, m * chunk : (m + 1) * chunk, :] = value

    def group(g, carry):
        rolled[...] = pltpu.roll(columns[...], 128 - g * UNROLL, 1)
        for j in range(UNROLL):
            pair = g * UNROLL + j
            picked = pl.ds(pair, 8, stride=PAIRS)
            left = jnp.concatenate([wide[tile, picked, :] for tile in range(TILES)], axis=1)
            left = left.astype(jnp.bfloat16)
            mine = rows[pl.ds(pair, 1), :].astype(jnp.bfloat16)
            accs = []
            for n in range(3):
                if start_refs is None:
                    accs.append(jnp.zeros((8, 256), jnp.float32))
                else:
                    accs.append(
                        jnp.concatenate(
                            [start_refs[0][2 * n + i, picked, :] for i in range(2)], axis=1
                        )
                    )
            for k in range(3):
                low = k * 256
                size = min(256, DEPTH - low)
                theirs = jnp.broadcast_to(rolled[low : low + size, j : j + 1], (size, 128))
                theirs = theirs.astype(jnp.bfloat16)
                theirs = jnp.concatenate([theirs, theirs], axis=1)
                for n in range(3):
                    lanes = slice(n * 256, (n + 1) * 256)
                    apart = jnp.broadcast_to(mine[:, lanes], (size, 256)) - theirs
                    sign = jnp.minimum(
                        jnp.maximum(apart, negative[low : low + size, lanes]),
                        compat[low : low + size, lanes],
                    )
                    accs[n] += jnp.dot(
                        left[:, low : low + size], sign, preferred_element_type=jnp.float32
                    )
            for n in range(3):
                for i in range(2):
                    show_ref[2 * n + i, picked, :] = accs[n][:, i * 128 : (i + 1) * 128]
        return carry

    lax.fori_loop(0, PAIRS // UNROLL, group, 0)


def settle_kernel(
    turn_ref,
    pot_ref,
    bet_ref,
    river_ref,
    cards_ref,
    first_ref,
    second_ref,
    show_ref,
    contact_ref,
    values_ref,
    new_first_ref,
    new_second_ref,
):
    hand = lax.axis_index("hand")
    flat = second_ref.reshape(PAIRS * 4, 128)
    new_flat = new_second_ref.reshape(PAIRS * 4, 128)
    for turn in range(TURNS_HERE):
        alive = alive_rows(cards_ref, turn_ref, river_ref, hand, turn).astype(jnp.float32)
        pot = jnp.full((1, 128), pot_ref[turn], jnp.int32).astype(jnp.float32)
        share = [
            0.5 + jnp.full((1, 128), bet_ref[turn, b], jnp.int32).astype(jnp.float32) / pot
            for b in range(2)
        ]

        def show(c):
            start = c * PAIRS + turn * RIVERS_HERE
            return show_ref[0, start : start + RIVERS_HERE, :]

        def contact(c):
            start = c * PAIRS + turn * RIVERS_HERE
            return contact_ref[0, start : start + RIVERS_HERE, :]

        base = contact(0)
        utility = [
            0.5 * show(0) * alive,
            (0.5 * (base - contact(1)) + share[0] * show(1)) * alive,
            (0.5 * (base - contact(2)) + share[1] * show(2)) * alive,
        ]
        actions = [first_ref[turn, a] for a in range(3)]
        total = actions[0] + actions[1] + actions[2]
        v1 = (
            actions[0] / total * utility[0]
            + actions[1] / total * utility[1]
            + actions[2] / total * utility[2]
        )
        for a in range(3):
            new_first_ref[turn, a] = jnp.maximum(actions[a] + utility[a] - v1, 0.0)
        v2 = 0.5 * show(3) * alive
        for b in range(2):
            fold, call = second_rows(flat, turn, b)
            prob = call / (fold + call)
            fold_value = -0.5 * contact(4 + b) * alive
            call_value = share[b] * show(4 + b) * alive
            node = (1.0 - prob) * fold_value + prob * call_value
            v2 = v2 + node
            row = turn * RIVERS_HERE * 4 + 2 * b
            new_flat[pl.ds(row, RIVERS_HERE, stride=4), :] = jnp.maximum(
                fold + fold_value - node, 0.0
            )
            new_flat[pl.ds(row + 1, RIVERS_HERE, stride=4), :] = jnp.maximum(
                call + call_value - node, 0.0
            )
        values_ref[turn, 0:1, :] = jnp.sum(v1, axis=0, keepdims=True)
        values_ref[turn, 1:2, :] = jnp.sum(v2, axis=0, keepdims=True)


def whole(space=pltpu.VMEM):
    return pl.BlockSpec(memory_space=space)


def tiled(*shape):
    count = len(shape)
    return pl.BlockSpec(shape + (128,), lambda tile: (0,) * count + (tile,))


def planes(rows):
    return pl.BlockSpec((1, rows, 128), lambda tile: (tile, 0, 0))


def sums(slot, ranks, operands, table, starts):
    return pl.pallas_call(
        functools.partial(sums_kernel, slot),
        out_shape=(
            jax.ShapeDtypeStruct((TILES, 8 * PAIRS, 128), jnp.float32),
            jax.ShapeDtypeStruct((TILES, 6 * PAIRS, 128), jnp.float32),
        ),
        in_specs=[whole(), whole(), whole(pl.ANY)] + [whole()] * len(starts),
        out_specs=(whole(), whole()),
        scratch_shapes=[
            pltpu.VMEM((WIDTH, WIDTH), jnp.bfloat16),
            pltpu.VMEM((WIDTH, WIDTH), jnp.bfloat16),
            pltpu.VMEM((PAIRS, WIDTH), jnp.float32),
            pltpu.VMEM((128, WIDTH), jnp.float32),
            pltpu.VMEM((WIDTH, 128), jnp.float32),
            pltpu.VMEM((WIDTH, 128), jnp.float32),
            pltpu.VMEM((TILES, 8 * PAIRS, 128), jnp.float32),
            pltpu.SemaphoreType.DMA,
        ],
        compiler_params=pltpu.CompilerParams(vmem_limit_bytes=VMEM_LIMIT),
        cost_estimate=pl.CostEstimate(
            flops=2 * PAIRS * 256 * DEPTH * WIDTH, bytes_accessed=1 << 23, transcendentals=0
        ),
    )(ranks, operands, table, *starts)


def swapped(value, axis, size, step):
    return lax.ppermute(value, axis, [(i, i ^ step) for i in range(size)])


def shards(
    reach_probs,
    turn_cards,
    river_cards,
    hand_ranks,
    pot_chips,
    bet_chips,
    regrets_first,
    regrets_second,
):
    halves, compat = card_tables()
    cards = jnp.asarray(halves)
    table = jnp.asarray(compat).astype(jnp.bfloat16)
    ranks = hand_ranks.reshape(PAIRS, HANDS)
    first = jnp.transpose(regrets_first, (0, 2, 1, 3))
    second = regrets_second.reshape(PAIRS, 4, HALF)
    params = pltpu.CompilerParams(vmem_limit_bytes=VMEM_LIMIT)

    operands = pl.pallas_call(
        operand_kernel,
        grid=(TILES,),
        out_shape=jax.ShapeDtypeStruct((TILES, 6 * PAIRS, 128), jnp.bfloat16),
        in_specs=[
            whole(pltpu.SMEM),
            whole(),
            tiled(2, 2),
            tiled(TURNS_HERE, 2),
            tiled(TURNS_HERE, 3, RIVERS_HERE),
            tiled(PAIRS, 4),
        ],
        out_specs=planes(6 * PAIRS),
        compiler_params=params,
        cost_estimate=pl.CostEstimate(flops=1 << 22, bytes_accessed=1 << 22, transcendentals=0),
    )(turn_cards, river_cards, cards, reach_probs, first, second)

    others = swapped(operands, "hand", 2, 1)
    started = sums(0, ranks, operands, table, ())
    show, contact = sums(1, ranks, others, table, started)

    partial, new_first, new_second = pl.pallas_call(
        settle_kernel,
        grid=(TILES,),
        out_shape=(
            jax.ShapeDtypeStruct((TURNS_HERE, 2, HALF), jnp.float32),
            jax.ShapeDtypeStruct(first.shape, jnp.float32),
            jax.ShapeDtypeStruct(second.shape, jnp.float32),
        ),
        in_specs=[
            whole(pltpu.SMEM),
            whole(pltpu.SMEM),
            whole(pltpu.SMEM),
            whole(),
            tiled(2, 2),
            tiled(TURNS_HERE, 3, RIVERS_HERE),
            tiled(PAIRS, 4),
            planes(8 * PAIRS),
            planes(6 * PAIRS),
        ],
        out_specs=(
            tiled(TURNS_HERE, 2),
            tiled(TURNS_HERE, 3, RIVERS_HERE),
            tiled(PAIRS, 4),
        ),
        compiler_params=params,
        cost_estimate=pl.CostEstimate(flops=1 << 23, bytes_accessed=1 << 23, transcendentals=0),
    )(
        turn_cards,
        pot_chips,
        bet_chips,
        river_cards,
        cards,
        first,
        second,
        show,
        contact,
    )

    turn_values = (partial + swapped(partial, "river", 2, 1)) / RIVERS
    flop_values = jnp.sum(turn_values, axis=0)
    for axis, size in (("y", 4), ("xh", 2), ("z", 8)):
        step = 1
        while step < size:
            flop_values = flop_values + swapped(flop_values, axis, size, step)
            step *= 2
    return (
        turn_values,
        flop_values,
        jnp.transpose(new_first, (0, 2, 1, 3)),
        new_second.reshape(regrets_second.shape),
    )


def solution(mesh):
    board = ("z", "xh", "y")
    split = Mesh(mesh.devices.reshape(8, 2, 4, 2, 2), board + ("river", "hand"))
    placed = (
        P(board, None, "hand"),
        P(board, None),
        P(board, "river"),
        P(board, "river", None),
        P(board),
        P(board, None),
        P(board, "river", None, "hand"),
        P(board, "river", None, "hand"),
    )
    return jax.shard_map(
        shards,
        mesh=split,
        in_specs=placed,
        out_specs=(
            P(board, None, "hand"),
            P(None, "hand"),
            P(board, "river", None, "hand"),
            P(board, "river", None, "hand"),
        ),
        check_vma=False,
    )
```

time: 415 us -> 105 us (0.25)
  blocking collectives: 190 us -> 0 us
  matrix products: 93.7 us -> 0 us
  local copies, waits for them, and re-layouts: 72.5 us -> 1.58 us
  Pallas kernels: 0 us -> 66.8 us
  between operations: 14.3 us -> 0.68 us
  starting transfers between devices: 0.04 us -> 11.6 us
  waiting for transfers between devices: 32.3 us -> 21.7 us
  other arithmetic: 9.36 us -> 1.99 us
    psum x2 -> x0, blocking collectives: 190 us -> none  [the longest x1 187 us: shards(): flop_values = lax.psum(jnp.sum(turn_values, axis=0), 'board')]
    dot_general x15 -> x0, matrix products: 93.7 us -> none  [the longest x12 86.8 us: per_block(): lax.dot_general(rows_six, signed, batched, preferred_element_type=jnp.flo...]
    pallas_call x0 -> x4, Pallas kernels: none -> 66.8 us  [the longest x2 55.6 us: sums(): pl.pallas_call(functools.partial(sums_kernel, slot), out_shape=(jax.Shape...]
    all_gather x1 -> x0, waiting for transfers between devices: 32.3 us -> none  [shards(): block_rows = lax.all_gather(operand_flat, 'hand', axis=1, tiled=True)]
    slice x3 -> x0, local copies, waits for them, and re-layouts: 24.8 us -> none  [the longest x1 9.33 us: shards(): regrets_second[:, :, 1::2]]
    ppermute x0 -> x8, waiting for transfers between devices: none -> 21.7 us  [swapped(): return lax.ppermute(value, axis, [(i, i ^ step) for i in range(size)])]
    gt x24 -> x0, local copies, waits for them, and re-layouts: 18.4 us -> none  [signed_table(): first_ranks[:, :, None] > second_ranks[:, None, :]]
    ppermute x0 -> x8, starting transfers between devices: none -> 11.6 us  [swapped(): return lax.ppermute(value, axis, [(i, i ^ step) for i in range(size)])]
  transfers between devices with their start and end apart: 1 -> 8, of which waited for: 1 -> 7; matrix products, arithmetic and copies ran while one was open for 1% -> 1% of each run, Pallas kernels for 0% -> 27%
where the time goes in v1:
time: 105 us; the launch traced here: 104 us
  Pallas kernels  66.8 us (64%)
  waiting for transfers between devices  21.7 us (21%)
  starting transfers between devices  11.6 us (11%)
  other arithmetic  1.99 us (2%)
  local copies, waits for them, and re-layouts  1.58 us (2%)
    pallas_call x2, Pallas kernels, sums(): pl.pallas_call(functools.partial(sums_kernel, slot), out_shape=(jax.Shape...  55.6 us
    ppermute x8, waiting for transfers between devices, swapped(): return lax.ppermute(value, axis, [(i, i ^ step) for i in range(size)])  21.7 us
    ppermute x8, starting transfers between devices, swapped(): return lax.ppermute(value, axis, [(i, i ^ step) for i in range(size)])  11.6 us
    pallas_call x1, Pallas kernels, shards(): pl.pallas_call(settle_kernel, grid=(TILES,), out_shape=(jax.ShapeDtypeStr...  6.14 us
    pallas_call x1, Pallas kernels, shards(): pl.pallas_call(operand_kernel, grid=(TILES,), out_shape=jax.ShapeDtypeStr...  5.03 us
  transfers between devices with their start and end apart: 8, of which 7 were waited for; matrix products, arithmetic and copies ran while one was open for 1% of the time, Pallas kernels for 27%

profile of v1, /device:TPU:2, one launch (start us, length us, event | category | flops | bytes accessed | tf_op | source)
XLA Modules:
  0.0 104.4 jit_solution(2394552954508326522)
XLA Ops:
  0.6 5.0 %shard_map.129.ops_ref = bf16[6,576,128]{2,1,0:T(8,128)(2,1)} custom-call(s32[4,4]{1,0:T(4,128)} %turn_ref.3, s32[4,24]{1,0:T(4,128)} %river_ref.3, s32[2,2,768]{2,1,0:T(2,128)} %constant.9.clone.cards_ref, f32[4,2,663]{2,1,0:T(2,128)} %reach_ref.1, f32[4,3,24,663]{3,2,1,0:T(8,128)} %bitcast.7, f32[96,4,663]{2,1,0:T(4,128)} %bitcast.5), custom_call_target="tpu_custom_call" | custom-call | flops 4194304 | bytes 4194304 | tf_op jit(solution)/shard_map/pallas_call | solution.py:323
  5.7 2.3 %collective-permute-start = (bf16[6,576,128]{2,1,0:T(8,128)(2,1)}, bf16[6,576,128]{2,1,0:T(8,128)(2,1)S(1)}, u32[]{:S(2)}, u32[]{:S(2)}) collective-permute-start(bf16[6,576,128]{2,1,0:T(8,128)(2,1)} %shard_map.129.ops_ref), channel_id=1, source_target_pairs={{0,1},{1,0},{2,3},{3,2},{4,5},{5,4},{6,7},{7,6},{8,9},{9,8},{10,11... | collective-permute-start | bytes 2654216 | tf_op jit(solution)/shard_map/ppermute | solution.py:302
  7.9 27.9 %shard_map.130 = (f32[6,768,128]{2,1,0:T(8,128)}, f32[6,576,128]{2,1,0:T(8,128)}) custom-call(s32[96,1326]{1,0:T(8,128)} %bitcast.11, bf16[6,576,128]{2,1,0:T(8,128)(2,1)} %shard_map.129.ops_ref, bf16[2,2,768,768]{3,2,1,0:T(8,128)(2,1)} %constant.19.table_ref), custom_call_target="tpu_custom_call" | custom-call | flops 25367150592 | bytes 8388608 | tf_op jit(solution)/shard_map/pallas_call | solution.py:276
  35.9 0.7 copy.14.bet_ref
  36.5 0.0 collective-permute-done.ops_ref
  36.5 0.9 copy-done.1
  37.5 27.7 %shard_map.131 = (f32[6,768,128]{2,1,0:T(8,128)}, f32[6,576,128]{2,1,0:T(8,128)}) custom-call(s32[96,1326]{1,0:T(8,128)} %bitcast.12, bf16[6,576,128]{2,1,0:T(8,128)(2,1)} %copy-done.1, bf16[2,2,768,768]{3,2,1,0:T(8,128)(2,1)} %constant.19.table_ref, f32[6,768,128]{2,1,0:T(8,128)} %get-tuple-element.11.refs_0_, f32[6,576,128]{2,1,0:T(8,128)} %get-tuple-element.12.refs_1_), custom_call_target="tpu_custom_call" | custom-call | flops 25367150592 | bytes 8388608 | tf_op jit(solution)/shard_map/pallas_call | solution.py:276
  65.1 6.1 %shard_map.132 = (f32[4,2,663]{2,1,0:T(2,128)}, f32[4,3,24,663]{3,2,1,0:T(8,128)}, f32[96,4,663]{2,1,0:T(4,128)}) custom-call(s32[4,4]{1,0:T(4,128)} %turn_ref.3, s32[4]{0:T(128)} %pot_ref.1, s32[4,2]{1,0:T(4,128)} %copy.14.bet_ref, s32[4,24]{1,0:T(4,128)} %river_ref.3, s32[2,2,768]{2,1,0:T(2,128)} %constant.9.clone.cards_ref, f32[4,3,24,663]{3,2,1,0:T(8,128)} %bitcast.8, ...), custom_call_target="tpu_custom_call" | custom-call | flops 8388608 | bytes 8388608 | tf_op jit(solution)/shard_map/pallas_call | solution.py:344
  71.3 0.1 collective-permute-start.1
  71.4 1.4 %collective-permute-done.1 = f32[4,2,663]{2,1,0:T(2,128)S(1)} collective-permute-done((f32[4,2,663]{2,1,0:T(2,128)}, f32[4,2,663]{2,1,0:T(2,128)S(1)}, u32[]{:S(2)}, u32[]{:S(2)}) %collective-permute-start.1) | collective-permute-done | bytes 21248 | tf_op jit(solution)/shard_map/ppermute | solution.py:302
  72.8 1.4 %fusion = (f32[2,663]{1,0:T(2,128)S(1)}, f32[4,2,663]{2,1,0:T(2,128)}) fusion(f32[4,2,663]{2,1,0:T(2,128)} %get-tuple-element.15, f32[4,2,663]{2,1,0:T(2,128)S(1)} %collective-permute-done.1), kind=kLoop, calls=%fused_computation.1 | loop fusion | flops 14586 | bytes 68952 | tf_op jit(solution)/shard_map/reduce_sum | solution.py:383
  74.1 0.0 collective-permute-start.2
  74.1 3.6 %collective-permute-done.2 = f32[2,663]{1,0:T(2,128)S(1)} collective-permute-done((f32[2,663]{1,0:T(2,128)S(1)}, f32[2,663]{1,0:T(2,128)S(1)}, u32[]{:S(2)}, u32[]{:S(2)}) %collective-permute-start.2) | collective-permute-done | bytes 5336 | tf_op jit(solution)/shard_map/ppermute | solution.py:302
  77.8 1.5 %collective-permute-start.3 = (f32[2,663]{1,0:T(2,128)S(1)}, f32[2,663]{1,0:T(2,128)S(1)}, u32[]{:S(2)}, u32[]{:S(2)}) collective-permute-start(f32[2,663]{1,0:T(2,128)S(1)} %add.22), channel_id=1, source_target_pairs={{0,8},{4,12},{8,0},{12,4},{1,9},{5,13},{9,1},{13,5},{2,10},{6,14},... | collective-permute-start | bytes 15920 | tf_op jit(solution)/shard_map/ppermute | solution.py:302
  79.2 3.7 %collective-permute-done.3 = f32[2,663]{1,0:T(2,128)S(1)} collective-permute-done((f32[2,663]{1,0:T(2,128)S(1)}, f32[2,663]{1,0:T(2,128)S(1)}, u32[]{:S(2)}, u32[]{:S(2)}) %collective-permute-start.3) | collective-permute-done | bytes 5336 | tf_op jit(solution)/shard_map/ppermute | solution.py:302
  82.9 0.7 collective-permute-start.4
  83.6 4.5 %collective-permute-done.4 = f32[2,663]{1,0:T(2,128)S(1)} collective-permute-done((f32[2,663]{1,0:T(2,128)S(1)}, f32[2,663]{1,0:T(2,128)S(1)}, u32[]{:S(2)}, u32[]{:S(2)}) %collective-permute-start.4) | collective-permute-done | bytes 5336 | tf_op jit(solution)/shard_map/ppermute | solution.py:302
  88.0 0.2 collective-permute-start.5
  88.2 3.4 %collective-permute-done.5 = f32[2,663]{1,0:T(2,128)S(1)} collective-permute-done((f32[2,663]{1,0:T(2,128)S(1)}, f32[2,663]{1,0:T(2,128)S(1)}, u32[]{:S(2)}, u32[]{:S(2)}) %collective-permute-start.5) | collective-permute-done | bytes 5336 | tf_op jit(solution)/shard_map/ppermute | solution.py:302
  91.7 1.5 %collective-permute-start.6 = (f32[2,663]{1,0:T(2,128)S(1)}, f32[2,663]{1,0:T(2,128)S(1)}, u32[]{:S(2)}, u32[]{:S(2)}) collective-permute-start(f32[2,663]{1,0:T(2,128)S(1)} %add.25), channel_id=1, source_target_pairs={{0,64},{32,96},{64,0},{96,32},{128,192},{160,224},{192,128},{224,1... | collective-permute-start | bytes 15920 | tf_op jit(solution)/shard_map/ppermute | solution.py:302
  93.2 3.0 %collective-permute-done.6 = f32[2,663]{1,0:T(2,128)S(1)} collective-permute-done((f32[2,663]{1,0:T(2,128)S(1)}, f32[2,663]{1,0:T(2,128)S(1)}, u32[]{:S(2)}, u32[]{:S(2)}) %collective-permute-start.6) | collective-permute-done | bytes 5336 | tf_op jit(solution)/shard_map/ppermute | solution.py:302
  96.2 5.4 %collective-permute-start.7 = (f32[2,663]{1,0:T(2,128)S(1)}, f32[2,663]{1,0:T(2,128)S(1)}, u32[]{:S(2)}, u32[]{:S(2)}) collective-permute-start(f32[2,663]{1,0:T(2,128)S(1)} %add.26), channel_id=1, source_target_pairs={{0,128},{32,160},{64,192},{96,224},{128,0},{160,32},{192,64},{224,... | collective-permute-start | bytes 15920 | tf_op jit(solution)/shard_map/ppermute | solution.py:302
  101.7 2.1 %collective-permute-done.7 = f32[2,663]{1,0:T(2,128)S(1)} collective-permute-done((f32[2,663]{1,0:T(2,128)S(1)}, f32[2,663]{1,0:T(2,128)S(1)}, u32[]{:S(2)}, u32[]{:S(2)}) %collective-permute-start.7) | collective-permute-done | bytes 5336 | tf_op jit(solution)/shard_map/ppermute | solution.py:302
  103.8 0.6 add.27
  (8 shorter events, 0.0 us)
Async XLA Ops:
  5.7 30.9 %collective-permute-start = (bf16[6,576,128]{2,1,0:T(8,128)(2,1)}, bf16[6,576,128]{2,1,0:T(8,128)(2,1)S(1)}, u32[]{:S(2)}, u32[]{:S(2)}) collective-permute-start(bf16[6,576,128]{2,1,0:T(8,128)(2,1)} %shard_map.129.ops_ref), channel_id=1, source_target_pairs={{0,1},{1,0},{2,3},{3,2},{4,5},{5,4},{6,7},{7,6},{8,9},{9,8},{10,11... | collective-permute-start | bytes 2654216 | tf_op jit(solution)/shard_map/ppermute | solution.py:302
  7.9 27.9 %copy-start = (s32[4,2]{0,1:T(2,128)S(1)}, s32[4,2]{0,1:T(2,128)}, u32[]{:S(2)}) copy-start(s32[4,2]{0,1:T(2,128)} %param.15) | copy-start | bytes 100
  36.5 0.9 copy-start.1
  71.3 1.5 %collective-permute-start.1 = (f32[4,2,663]{2,1,0:T(2,128)}, f32[4,2,663]{2,1,0:T(2,128)S(1)}, u32[]{:S(2)}, u32[]{:S(2)}) collective-permute-start(f32[4,2,663]{2,1,0:T(2,128)} %get-tuple-element.15), channel_id=1, source_target_pairs={{0,2},{2,0},{1,3},{3,1},{4,6},{6,4},{5,7},{7,5},{8,10},{10,8},{9,1... | collective-permute-start | bytes 63656 | tf_op jit(solution)/shard_map/ppermute | solution.py:302
  74.1 3.6 %collective-permute-start.2 = (f32[2,663]{1,0:T(2,128)S(1)}, f32[2,663]{1,0:T(2,128)S(1)}, u32[]{:S(2)}, u32[]{:S(2)}) collective-permute-start(f32[2,663]{1,0:T(2,128)S(1)} %get-tuple-element.18), channel_id=1, source_target_pairs={{0,4},{4,0},{8,12},{12,8},{1,5},{5,1},{9,13},{13,9},{2,6},{6,2},{1... | collective-permute-start | bytes 15920 | tf_op jit(solution)/shard_map/ppermute | solution.py:302
  77.8 5.1 %collective-permute-start.3 = (f32[2,663]{1,0:T(2,128)S(1)}, f32[2,663]{1,0:T(2,128)S(1)}, u32[]{:S(2)}, u32[]{:S(2)}) collective-permute-start(f32[2,663]{1,0:T(2,128)S(1)} %add.22), channel_id=1, source_target_pairs={{0,8},{4,12},{8,0},{12,4},{1,9},{5,13},{9,1},{13,5},{2,10},{6,14},... | collective-permute-start | bytes 15920 | tf_op jit(solution)/shard_map/ppermute | solution.py:302
  82.9 5.1 %collective-permute-start.4 = (f32[2,663]{1,0:T(2,128)S(1)}, f32[2,663]{1,0:T(2,128)S(1)}, u32[]{:S(2)}, u32[]{:S(2)}) collective-permute-start(f32[2,663]{1,0:T(2,128)S(1)} %add.23), channel_id=1, source_target_pairs={{0,16},{16,0},{1,17},{17,1},{2,18},{18,2},{3,19},{19,3},{4,20},{20... | collective-permute-start | bytes 15920 | tf_op jit(solution)/shard_map/ppermute | solution.py:302
  88.0 3.6 %collective-permute-start.5 = (f32[2,663]{1,0:T(2,128)S(1)}, f32[2,663]{1,0:T(2,128)S(1)}, u32[]{:S(2)}, u32[]{:S(2)}) collective-permute-start(f32[2,663]{1,0:T(2,128)S(1)} %add.24), channel_id=1, source_target_pairs={{0,32},{32,0},{64,96},{96,64},{128,160},{160,128},{192,224},{224,1... | collective-permute-start | bytes 15920 | tf_op jit(solution)/shard_map/ppermute | solution.py:302
  91.7 4.6 %collective-permute-start.6 = (f32[2,663]{1,0:T(2,128)S(1)}, f32[2,663]{1,0:T(2,128)S(1)}, u32[]{:S(2)}, u32[]{:S(2)}) collective-permute-start(f32[2,663]{1,0:T(2,128)S(1)} %add.25), channel_id=1, source_target_pairs={{0,64},{32,96},{64,0},{96,32},{128,192},{160,224},{192,128},{224,1... | collective-permute-start | bytes 15920 | tf_op jit(solution)/shard_map/ppermute | solution.py:302
  96.2 7.5 %collective-permute-start.7 = (f32[2,663]{1,0:T(2,128)S(1)}, f32[2,663]{1,0:T(2,128)S(1)}, u32[]{:S(2)}, u32[]{:S(2)}) collective-permute-start(f32[2,663]{1,0:T(2,128)S(1)} %add.26), channel_id=1, source_target_pairs={{0,128},{32,160},{64,192},{96,224},{128,0},{160,32},{192,64},{224,... | collective-permute-start | bytes 15920 | tf_op jit(solution)/shard_map/ppermute | solution.py:302

commit v2 on v1

v2 whole, which is shorter than its diff:
```python
import functools

import jax
import jax.numpy as jnp
import numpy as np
from jax import lax
from jax.experimental import pallas as pl
from jax.experimental.pallas import tpu as pltpu
from jax.sharding import Mesh
from jax.sharding import PartitionSpec as P

DECK = 52
HANDS = 1326
RIVERS = 48
HALF = HANDS // 2
TILES = 6
WIDTH = TILES * 128
DEPTH = 672
TURNS_HERE = 4
RIVERS_HERE = 24
PAIRS = TURNS_HERE * RIVERS_HERE
UNROLL = 32
STEP_TILES = 3
VMEM_LIMIT = 24 << 20
VMEM_ALONE = 56 << 20


def card_tables():
    lower, upper = np.triu_indices(DECK, 1)
    halves = np.full((2, 2, WIDTH), -1, np.int32)
    for half in range(2):
        halves[half, 0, :HALF] = lower[half * HALF : (half + 1) * HALF]
        halves[half, 1, :HALF] = upper[half * HALF : (half + 1) * HALF]
    compat = np.zeros((2, 2, WIDTH, WIDTH), np.float32)
    for own in range(2):
        for slot in range(2):
            other = own ^ slot
            shares = np.zeros((WIDTH, WIDTH), bool)
            for i in range(2):
                for j in range(2):
                    shares |= halves[other, i][:, None] == halves[own, j][None, :]
            compat[own, slot, :HALF, :HALF] = ~shares[:HALF, :HALF]
    return halves, compat


def alive_rows(cards_ref, turn_ref, river_ref, hand, turn):
    low = jnp.where(hand == 0, cards_ref[0, 0:1, :], cards_ref[1, 0:1, :])
    high = jnp.where(hand == 0, cards_ref[0, 1:2, :], cards_ref[1, 1:2, :])
    good = low >= 0
    for k in range(4):
        dead = turn_ref[turn, k]
        good = good & (low != dead) & (high != dead)
    row = jnp.broadcast_to(river_ref[turn : turn + 1, :], (RIVERS_HERE, RIVERS_HERE))
    diagonal = lax.broadcasted_iota(jnp.int32, row.shape, 0) == lax.broadcasted_iota(
        jnp.int32, row.shape, 1
    )
    column = jnp.sum(jnp.where(diagonal, row, 0), axis=1, keepdims=True)
    column = jnp.broadcast_to(column, (RIVERS_HERE, 128))
    low = jnp.broadcast_to(low, column.shape)
    high = jnp.broadcast_to(high, column.shape)
    good = jnp.broadcast_to(good.astype(jnp.int32), column.shape)
    return (good > 0) & (low != column) & (high != column)


def second_rows(flat, turn, b):
    base = turn * RIVERS_HERE * 4 + 2 * b
    fold = flat[pl.ds(base, RIVERS_HERE, stride=4), :]
    call = flat[pl.ds(base + 1, RIVERS_HERE, stride=4), :]
    return fold, call


def operand_kernel(turn_ref, river_ref, *refs):
    hand = lax.axis_index("hand")
    scaling = 2.0 / HANDS
    out_ref = refs[-1]
    for tile in range(STEP_TILES):
        cards_ref, reach_ref, first_ref, second_ref = refs[tile:-1:STEP_TILES]
        flat = second_ref.reshape(PAIRS * 4, 128)
        for two in range(TURNS_HERE // 2):
            parts = []
            for turn in (2 * two, 2 * two + 1):
                alive = alive_rows(cards_ref, turn_ref, river_ref, hand, turn)
                x = jnp.where(alive, reach_ref[turn, 0:1, :] * scaling, 0.0)
                y = jnp.where(alive, reach_ref[turn, 1:2, :] * scaling, 0.0)
                actions = [first_ref[turn, a] for a in range(3)]
                total = actions[0] + actions[1] + actions[2]
                rows = [y]
                for b in range(2):
                    fold, call = second_rows(flat, turn, b)
                    rows.append(jnp.where(alive, y * (call / (fold + call)), 0.0))
                for a in range(3):
                    rows.append(jnp.where(alive, x * (actions[a] / total), 0.0))
                parts.append(rows)
            for c in range(6):
                both = jnp.concatenate([parts[0][c], parts[1][c]], axis=0)
                start = c * PAIRS + two * 2 * RIVERS_HERE
                out_ref[tile, start : start + 2 * RIVERS_HERE, :] = both.astype(jnp.bfloat16)


def ordered(ranks):
    return lax.shift_left((ranks & 127) + 128, lax.shift_right_logical(ranks, 7)).astype(
        jnp.float32
    )


def opposing_sums(slot, ranks_ref, ops_ref, table_ref, show_ref, contact_ref, scratch):
    compat, negative, rows, staged, columns, rolled, wide, sem = scratch
    hand = lax.axis_index("hand")
    fetch = pltpu.make_async_copy(table_ref.at[hand, slot], compat, sem)
    fetch.start()

    lower = ordered(ranks_ref[:, :HALF])
    upper = ordered(ranks_ref[:, HALF:])
    rows[...] = jnp.zeros_like(rows)
    staged[...] = jnp.zeros_like(staged)
    rows[:, :HALF] = jnp.where(hand == 0, lower, upper)
    staged[:PAIRS, :HALF] = jnp.where(hand == slot, lower, upper)
    for tile in range(TILES):
        columns[tile * 128 : (tile + 1) * 128, :] = staged[:, tile * 128 : (tile + 1) * 128].T
        wide[tile, : 6 * PAIRS, :] = ops_ref[tile].astype(jnp.float32)
        wide[tile, 6 * PAIRS :, :] = jnp.zeros((2 * PAIRS, 128), jnp.float32)
    fetch.wait()
    negative[...] = -compat[...]

    chunk = 2 * PAIRS
    for m in range(3):
        for n in range(3):
            acc = jnp.zeros((chunk, 256), jnp.float32)
            for k in range(3):
                left = jnp.concatenate(
                    [ops_ref[2 * k + i, m * chunk : (m + 1) * chunk, :] for i in range(2)], axis=1
                )
                acc += jnp.dot(
                    left,
                    compat[k * 256 : (k + 1) * 256, n * 256 : (n + 1) * 256],
                    preferred_element_type=jnp.float32,
                )
            for i in range(2):
                contact_ref[2 * n + i, m * chunk : (m + 1) * chunk, :] = acc[
                    :, i * 128 : (i + 1) * 128
                ]

    def group(g, carry):
        rolled[...] = pltpu.roll(columns[...], 128 - g * UNROLL, 1)
        for j in range(UNROLL):
            pair = g * UNROLL + j
            picked = pl.ds(pair, 8, stride=PAIRS)
            left = jnp.concatenate([wide[tile, picked, :] for tile in range(TILES)], axis=1)
            left = left.astype(jnp.bfloat16)
            mine = rows[pl.ds(pair, 1), :].astype(jnp.bfloat16)
            accs = [jnp.zeros((8, 256), jnp.float32) for n in range(3)]
            for k in range(3):
                low = k * 256
                size = min(256, DEPTH - low)
                theirs = jnp.broadcast_to(rolled[low : low + size, j : j + 1], (size, 128))
                theirs = theirs.astype(jnp.bfloat16)
                theirs = jnp.concatenate([theirs, theirs], axis=1)
                for n in range(3):
                    lanes = slice(n * 256, (n + 1) * 256)
                    apart = jnp.broadcast_to(mine[:, lanes], (size, 256)) - theirs
                    sign = jnp.minimum(jnp.maximum(apart, jnp.bfloat16(-1)), jnp.bfloat16(1)) * compat[low : low + size, lanes]
                    accs[n] += jnp.dot(
                        left[:, low : low + size], sign, preferred_element_type=jnp.float32
                    )
            for n in range(3):
                for i in range(2):
                    show_ref[2 * n + i, picked, :] = accs[n][:, i * 128 : (i + 1) * 128]
        return carry

    lax.fori_loop(0, PAIRS // UNROLL, group, 0)


def own_kernel(ranks_ref, ops_ref, table_ref, show_ref, contact_ref, *scratch):
    opposing_sums(0, ranks_ref, ops_ref, table_ref, show_ref, contact_ref, scratch)


def final_kernel(
    turn_ref,
    pot_ref,
    bet_ref,
    river_ref,
    cards_ref,
    ranks_ref,
    ops_ref,
    table_ref,
    *refs,
):
    sources = refs[:4]
    values_ref, flop_ref, new_first_ref, new_second_ref = refs[4:8]
    show_other, contact_other, staged_in, staged_out = refs[8:12]
    held = refs[12:16]
    sems = refs[16:20]
    copies = [pltpu.make_async_copy(*each) for each in zip(sources, held, sems)]
    for copy in copies:
        copy.start()
    opposing_sums(1, ranks_ref, ops_ref, table_ref, show_other, contact_other, refs[20:])
    for copy in copies:
        copy.wait()
    show_own, contact_own, first_ref, second_ref = held
    for tile in range(TILES):
        settle(
            tile,
            turn_ref,
            pot_ref,
            bet_ref,
            river_ref,
            cards_ref,
            first_ref,
            second_ref,
            staged_in,
            staged_out,
            show_own.at[tile],
            show_other.at[tile],
            contact_own.at[tile],
            contact_other.at[tile],
            values_ref,
            flop_ref,
            new_first_ref,
            new_second_ref,
        )


def settle(
    tile,
    turn_ref,
    pot_ref,
    bet_ref,
    river_ref,
    cards_ref,
    first_ref,
    second_ref,
    staged_in,
    staged_out,
    show_own,
    show_other,
    contact_own,
    contact_other,
    values_ref,
    flop_ref,
    new_first_ref,
    new_second_ref,
):
    hand = lax.axis_index("hand")
    width = min(128, HALF - tile * 128)
    lanes = slice(tile * 128, tile * 128 + width)
    wide_lanes = slice(tile * 128, (tile + 1) * 128)
    staged_in[:, :, :width] = second_ref[:, :, lanes]
    flat = staged_in.reshape(PAIRS * 4, 128)
    new_flat = staged_out.reshape(PAIRS * 4, 128)
    for turn in range(TURNS_HERE):
        alive = alive_rows(cards_ref.at[:, :, wide_lanes], turn_ref, river_ref, hand, turn)
        alive = alive.astype(jnp.float32)
        pot = jnp.full((1, 128), pot_ref[turn], jnp.int32).astype(jnp.float32)
        share = [
            0.5 + jnp.full((1, 128), bet_ref[b, turn], jnp.int32).astype(jnp.float32) / pot
            for b in range(2)
        ]

        def rows_of(own, other, c):
            start = c * PAIRS + turn * RIVERS_HERE
            here = slice(start, start + RIVERS_HERE)
            return own[here, :] + other[here, :]

        show = functools.partial(rows_of, show_own, show_other)
        contact = functools.partial(rows_of, contact_own, contact_other)
        base = contact(0)
        utility = [
            0.5 * show(0) * alive,
            (0.5 * (base - contact(1)) + share[0] * show(1)) * alive,
            (0.5 * (base - contact(2)) + share[1] * show(2)) * alive,
        ]
        actions = [first_ref[turn, a, :, lanes] for a in range(3)]
        utility = [value[:, :width] for value in utility]
        total = actions[0] + actions[1] + actions[2]
        v1 = (
            actions[0] / total * utility[0]
            + actions[1] / total * utility[1]
            + actions[2] / total * utility[2]
        )
        for a in range(3):
            new_first_ref[turn, a, :, lanes] = jnp.maximum(actions[a] + utility[a] - v1, 0.0)
        v2 = 0.5 * show(3) * alive
        for b in range(2):
            fold, call = second_rows(flat, turn, b)
            prob = call / (fold + call)
            fold_value = -0.5 * contact(4 + b) * alive
            call_value = share[b] * show(4 + b) * alive
            node = (1.0 - prob) * fold_value + prob * call_value
            v2 = v2 + node
            row = turn * RIVERS_HERE * 4 + 2 * b
            new_flat[pl.ds(row, RIVERS_HERE, stride=4), :] = jnp.maximum(
                fold + fold_value - node, 0.0
            )
            new_flat[pl.ds(row + 1, RIVERS_HERE, stride=4), :] = jnp.maximum(
                call + call_value - node, 0.0
            )
        sums = (jnp.sum(v1, axis=0, keepdims=True), jnp.sum(v2, axis=0, keepdims=True)[:, :width])
        for player in range(2):
            values_ref[turn, player : player + 1, lanes] = sums[player]
        totals = sums if turn == 0 else [total + each for total, each in zip(totals, sums)]
    for player in range(2):
        flop_ref[player : player + 1, lanes] = totals[player] * (1.0 / RIVERS)
    new_second_ref[:, :, lanes] = staged_out[:, :, :width]


def whole(space=pltpu.VMEM):
    return pl.BlockSpec(memory_space=space)


def views(*shape):
    count = len(shape)
    return [
        pl.BlockSpec(
            shape + (128,), lambda step, tile=tile: (0,) * count + (step * STEP_TILES + tile,)
        )
        for tile in range(STEP_TILES)
    ]


def sum_scratch():
    return [
        pltpu.VMEM((WIDTH, WIDTH), jnp.bfloat16),
        pltpu.VMEM((WIDTH, WIDTH), jnp.bfloat16),
        pltpu.VMEM((PAIRS, WIDTH), jnp.float32),
        pltpu.VMEM((128, WIDTH), jnp.float32),
        pltpu.VMEM((WIDTH, 128), jnp.float32),
        pltpu.VMEM((WIDTH, 128), jnp.float32),
        pltpu.VMEM((TILES, 8 * PAIRS, 128), jnp.float32),
        pltpu.SemaphoreType.DMA,
    ]


def exchange(value, axis, *pairs):
    return lax.ppermute(value, axis, [p for a, b in pairs for p in ((a, b), (b, a))])


def shards(
    reach_probs,
    turn_cards,
    river_cards,
    hand_ranks,
    pot_chips,
    bet_chips,
    regrets_first,
    regrets_second,
):
    halves, compat = card_tables()
    cards = jnp.asarray(halves)
    table = jnp.asarray(compat).astype(jnp.bfloat16)
    ranks = hand_ranks.reshape(PAIRS, HANDS)
    first = jnp.transpose(regrets_first, (0, 2, 1, 3))
    second = regrets_second.reshape(PAIRS, 4, HALF)
    params = pltpu.CompilerParams(vmem_limit_bytes=VMEM_LIMIT)
    alone = pltpu.CompilerParams(vmem_limit_bytes=VMEM_ALONE)
    sums_cost = pl.CostEstimate(
        flops=2 * PAIRS * 256 * DEPTH * WIDTH, bytes_accessed=1 << 23, transcendentals=0
    )
    show_shape = (TILES, 8 * PAIRS, 128)
    contact_shape = (TILES, 6 * PAIRS, 128)

    operands = pl.pallas_call(
        operand_kernel,
        grid=(TILES // STEP_TILES,),
        out_shape=jax.ShapeDtypeStruct(contact_shape, jnp.bfloat16),
        in_specs=[whole(pltpu.SMEM), whole()]
        + views(2, 2)
        + views(TURNS_HERE, 2)
        + views(TURNS_HERE, 3, RIVERS_HERE)
        + views(PAIRS, 4),
        out_specs=pl.BlockSpec((STEP_TILES, 6 * PAIRS, 128), lambda step: (step, 0, 0)),
        compiler_params=alone,
        cost_estimate=pl.CostEstimate(flops=1 << 22, bytes_accessed=1 << 22, transcendentals=0),
    )(
        turn_cards,
        river_cards,
        *[cards] * STEP_TILES,
        *[reach_probs] * STEP_TILES,
        *[first] * STEP_TILES,
        *[second] * STEP_TILES,
    )

    others = exchange(operands, "hand", (0, 1))
    show, contact = pl.pallas_call(
        own_kernel,
        out_shape=(
            jax.ShapeDtypeStruct(show_shape, jnp.float32),
            jax.ShapeDtypeStruct(contact_shape, jnp.float32),
        ),
        in_specs=[whole(), whole(), whole(pl.ANY)],
        out_specs=(whole(), whole()),
        scratch_shapes=sum_scratch(),
        compiler_params=params,
        cost_estimate=sums_cost,
    )(ranks, operands, table)

    partial, flop_values, new_first, new_second = pl.pallas_call(
        final_kernel,
        out_shape=(
            jax.ShapeDtypeStruct((TURNS_HERE, 2, HALF), jnp.float32),
            jax.ShapeDtypeStruct((2, HALF), jnp.float32),
            jax.ShapeDtypeStruct(first.shape, jnp.float32),
            jax.ShapeDtypeStruct(second.shape, jnp.float32),
        ),
        in_specs=[whole(pltpu.SMEM)] * 3 + [whole()] * 4 + [whole(pl.ANY)] * 5,
        out_specs=(whole(), whole(), whole(), whole()),
        scratch_shapes=[
            pltpu.VMEM(show_shape, jnp.float32),
            pltpu.VMEM(contact_shape, jnp.float32),
            pltpu.VMEM((PAIRS, 4, 128), jnp.float32),
            pltpu.VMEM((PAIRS, 4, 128), jnp.float32),
            pltpu.VMEM(show_shape, jnp.float32),
            pltpu.VMEM(contact_shape, jnp.float32),
            pltpu.VMEM(first.shape, jnp.float32),
            pltpu.VMEM(second.shape, jnp.float32),
        ]
        + [pltpu.SemaphoreType.DMA] * 4
        + sum_scratch(),
        compiler_params=params,
        cost_estimate=sums_cost,
    )(
        turn_cards,
        pot_chips,
        bet_chips.T,
        river_cards,
        cards,
        ranks,
        others,
        table,
        show,
        contact,
        first,
        second,
    )

    for axis, pairs in (
        ("river", ((0, 1),)),
        ("y", ((0, 1), (2, 3))),
        ("y", ((0, 3), (1, 2))),
        ("xh", ((0, 1),)),
        ("z", ((0, 1), (2, 3), (4, 5), (6, 7))),
        ("z", ((1, 2), (3, 4), (5, 6), (7, 0))),
        ("z", ((2, 5), (1, 6), (0, 3), (4, 7))),
    ):
        flop_values = flop_values + exchange(flop_values, axis, *pairs)
    turn_values = (partial + exchange(partial, "river", (0, 1))) / RIVERS
    return (
        turn_values,
        flop_values,
        jnp.transpose(new_first, (0, 2, 1, 3)),
        new_second.reshape(regrets_second.shape),
    )


def solution(mesh):
    board = ("z", "xh", "y")
    split = Mesh(mesh.devices.reshape(8, 2, 4, 2, 2), board + ("river", "hand"))
    placed = (
        P(board, None, "hand"),
        P(board, None),
        P(board, "river"),
        P(board, "river", None),
        P(board),
        P(board, None),
        P(board, "river", None, "hand"),
        P(board, "river", None, "hand"),
    )
    return jax.shard_map(
        shards,
        mesh=split,
        in_specs=placed,
        out_specs=(
            P(board, None, "hand"),
            P(None, "hand"),
            P(board, "river", None, "hand"),
            P(board, "river", None, "hand"),
        ),
        check_vma=False,
    )
```

time: 105 us -> 79.5 us (0.76)
  Pallas kernels: 66.8 us -> 42.5 us
  starting transfers between devices: 11.6 us -> 18.9 us
  waiting for transfers between devices: 21.7 us -> 14.7 us
    pallas_call x4 -> x3, Pallas kernels: 66.8 us -> 42.5 us  [the longest x1 21.9 us: shards(): pl.pallas_call(final_kernel, out_shape=(jax.ShapeDtypeStruct((TURNS_HERE,...]
    ppermute x8 -> x9, starting transfers between devices: 11.6 us -> 18.9 us  [exchange(): lax.ppermute(value, axis, [p for a, b in pairs for p in ((a, b), (b, a))])]
    ppermute x8 -> x9, waiting for transfers between devices: 21.7 us -> 14.7 us  [exchange(): lax.ppermute(value, axis, [p for a, b in pairs for p in ((a, b), (b, a))])]
    reduce_sum x1 -> x0, other arithmetic: 1.37 us -> none  [shards(): flop_values = jnp.sum(turn_values, axis=0)]
  transfers between devices with their start and end apart: 8 -> 9, of which waited for: 7 -> 8; matrix products, arithmetic and copies ran while one was open for 1% -> 1% of each run, Pallas kernels for 27% -> 22%
where the time goes in v2:
time: 79.5 us; the launch traced here: 79.4 us
  Pallas kernels  42.5 us (53%)
  starting transfers between devices  18.9 us (24%)
  waiting for transfers between devices  14.7 us (18%)
  other arithmetic  1.25 us (2%)
  local copies, waits for them, and re-layouts  1.24 us (2%)
    pallas_call x1, Pallas kernels, shards(): pl.pallas_call(final_kernel, out_shape=(jax.ShapeDtypeStruct((TURNS_HERE,...  21.9 us
    ppermute x9, starting transfers between devices, exchange(): lax.ppermute(value, axis, [p for a, b in pairs for p in ((a, b), (b, a))])  18.9 us
    pallas_call x1, Pallas kernels, shards(): pl.pallas_call(own_kernel, out_shape=(jax.ShapeDtypeStruct(show_shape, jn...  17.6 us
    ppermute x9, waiting for transfers between devices, exchange(): lax.ppermute(value, axis, [p for a, b in pairs for p in ((a, b), (b, a))])  14.7 us
    pallas_call x1, Pallas kernels, shards(): pl.pallas_call(operand_kernel, grid=(TILES // STEP_TILES,), out_shape=jax...  3 us
  transfers between devices with their start and end apart: 9, of which 8 were waited for; matrix products, arithmetic and copies ran while one was open for 1% of the time, Pallas kernels for 22%

profile of v2, /device:TPU:2, one launch (start us, length us, event | category | flops | bytes accessed | tf_op | source)
XLA Modules:
  0.0 79.4 jit_solution(9391639667490524343)
XLA Ops:
  0.6 0.0 copy-start.9
  0.7 3.0 %shard_map.129.ops_ref = bf16[6,576,128]{2,1,0:T(8,128)(2,1)} custom-call(s32[4,4]{1,0:T(4,128)} %turn_ref.3, s32[4,24]{1,0:T(4,128)} %river_ref.3, s32[2,2,768]{2,1,0:T(2,128)} %constant.7.clone.refs_0_.refs_1_.refs_2_.cards_ref, s32[2,2,768]{2,1,0:T(2,128)} %constant.7.clone.refs_0_.refs_1_.refs_2_.cards_ref, ...), custom_call_target="tpu_custom_call" | custom-call | flops 4194304 | bytes 4194304 | tf_op jit(solution)/shard_map/pallas_call | solution.py:361
  3.7 2.4 %collective-permute-start = (bf16[6,576,128]{2,1,0:T(8,128)(2,1)}, bf16[6,576,128]{2,1,0:T(8,128)(2,1)S(1)}, u32[]{:S(2)}, u32[]{:S(2)}) collective-permute-start(bf16[6,576,128]{2,1,0:T(8,128)(2,1)} %shard_map.129.ops_ref), channel_id=1, source_target_pairs={{0,1},{1,0},{2,3},{3,2},{4,5},{5,4},{6,7},{7,6},{8,9},{9,8},{10,11... | collective-permute-start | bytes 2654216 | tf_op jit(solution)/shard_map/ppermute | solution.py:334
  6.0 1.2 %copy-done.2 = bf16[6,576,128]{2,1,0:T(8,128)(2,1)S(1)} copy-done((bf16[6,576,128]{2,1,0:T(8,128)(2,1)S(1)}, bf16[6,576,128]{2,1,0:T(8,128)(2,1)}, u32[]{:S(2)}) %copy-start.2) | copy-done | bytes 884760
  7.2 0.0 copy-start.5
  7.3 17.6 %shard_map.130 = (f32[6,768,128]{2,1,0:T(8,128)S(1)}, f32[6,576,128]{2,1,0:T(8,128)S(1)}) custom-call(s32[96,1326]{1,0:T(8,128)S(1)} %bitcast.14, bf16[6,576,128]{2,1,0:T(8,128)(2,1)S(1)} %copy-done.2, bf16[2,2,768,768]{3,2,1,0:T(8,128)(2,1)S(1)} %copy-done.9), custom_call_target="tpu_custom_call" | custom-call | flops 25367150592 | bytes 8388608 | tf_op jit(solution)/shard_map/pallas_call | solution.py:383
  24.8 0.5 collective-permute-done.ops_ref
  25.4 21.9 %shard_map.131 = (f32[4,2,663]{2,1,0:T(2,128)S(1)}, f32[2,663]{1,0:T(2,128)S(1)}, f32[4,3,24,663]{3,2,1,0:T(8,128)}, f32[96,4,663]{2,1,0:T(4,128)}) custom-call(s32[4,4]{1,0:T(4,128)S(1)} %copy-done.4, s32[4]{0:T(128)S(1)} %copy-done.8, s32[2,4]{1,0:T(2,128)S(1)} %bitcast.16, s32[4,24]{1,0:T(4,128)S(1)} %copy-done.5, s32[2,2,768]{2,1,0:T(2,128)S(1)} %copy-done.3, ...), custom_call_target="tpu_custom_call" | custom-call | flops 25367150592 | bytes 8388608 | tf_op jit(solution)/shard_map/pallas_call | solution.py:396
  47.3 0.1 collective-permute-start.2
  47.4 1.2 %collective-permute-done.2 = f32[2,663]{1,0:T(2,128)S(1)} collective-permute-done((f32[2,663]{1,0:T(2,128)S(1)}, f32[2,663]{1,0:T(2,128)S(1)}, u32[]{:S(2)}, u32[]{:S(2)}) %collective-permute-start.2) | collective-permute-done | bytes 5336 | tf_op jit(solution)/shard_map/ppermute | solution.py:334
  48.6 1.6 %collective-permute-start.3 = (f32[2,663]{1,0:T(2,128)S(1)}, f32[2,663]{1,0:T(2,128)S(1)}, u32[]{:S(2)}, u32[]{:S(2)}) collective-permute-start(f32[2,663]{1,0:T(2,128)S(1)} %add.25), channel_id=1, source_target_pairs={{0,4},{4,0},{8,12},{12,8},{1,5},{5,1},{9,13},{13,9},{2,6},{6,2},{1... | collective-permute-start | bytes 15920 | tf_op jit(solution)/shard_map/ppermute | solution.py:334
  50.2 2.1 %collective-permute-done.3 = f32[2,663]{1,0:T(2,128)S(1)} collective-permute-done((f32[2,663]{1,0:T(2,128)S(1)}, f32[2,663]{1,0:T(2,128)S(1)}, u32[]{:S(2)}, u32[]{:S(2)}) %collective-permute-start.3) | collective-permute-done | bytes 5336 | tf_op jit(solution)/shard_map/ppermute | solution.py:334
  52.2 3.0 %collective-permute-start.4 = (f32[2,663]{1,0:T(2,128)S(1)}, f32[2,663]{1,0:T(2,128)S(1)}, u32[]{:S(2)}, u32[]{:S(2)}) collective-permute-start(f32[2,663]{1,0:T(2,128)S(1)} %add.26), channel_id=1, source_target_pairs={{0,12},{12,0},{4,8},{8,4},{1,13},{13,1},{5,9},{9,5},{2,14},{14,2},... | collective-permute-start | bytes 15920 | tf_op jit(solution)/shard_map/ppermute | solution.py:334
  55.3 1.8 %collective-permute-done.4 = f32[2,663]{1,0:T(2,128)S(1)} collective-permute-done((f32[2,663]{1,0:T(2,128)S(1)}, f32[2,663]{1,0:T(2,128)S(1)}, u32[]{:S(2)}, u32[]{:S(2)}) %collective-permute-start.4) | collective-permute-done | bytes 5336 | tf_op jit(solution)/shard_map/ppermute | solution.py:334
  57.1 2.1 %collective-permute-start.5 = (f32[2,663]{1,0:T(2,128)S(1)}, f32[2,663]{1,0:T(2,128)S(1)}, u32[]{:S(2)}, u32[]{:S(2)}) collective-permute-start(f32[2,663]{1,0:T(2,128)S(1)} %add.27), channel_id=1, source_target_pairs={{0,16},{16,0},{1,17},{17,1},{2,18},{18,2},{3,19},{19,3},{4,20},{20... | collective-permute-start | bytes 15920 | tf_op jit(solution)/shard_map/ppermute | solution.py:334
  59.2 3.0 %collective-permute-done.5 = f32[2,663]{1,0:T(2,128)S(1)} collective-permute-done((f32[2,663]{1,0:T(2,128)S(1)}, f32[2,663]{1,0:T(2,128)S(1)}, u32[]{:S(2)}, u32[]{:S(2)}) %collective-permute-start.5) | collective-permute-done | bytes 5336 | tf_op jit(solution)/shard_map/ppermute | solution.py:334
  62.2 1.9 %collective-permute-start.6 = (f32[2,663]{1,0:T(2,128)S(1)}, f32[2,663]{1,0:T(2,128)S(1)}, u32[]{:S(2)}, u32[]{:S(2)}) collective-permute-start(f32[2,663]{1,0:T(2,128)S(1)} %add.28), channel_id=1, source_target_pairs={{0,32},{32,0},{64,96},{96,64},{128,160},{160,128},{192,224},{224,1... | collective-permute-start | bytes 15920 | tf_op jit(solution)/shard_map/ppermute | solution.py:334
  64.1 1.7 %collective-permute-done.6 = f32[2,663]{1,0:T(2,128)S(1)} collective-permute-done((f32[2,663]{1,0:T(2,128)S(1)}, f32[2,663]{1,0:T(2,128)S(1)}, u32[]{:S(2)}, u32[]{:S(2)}) %collective-permute-start.6) | collective-permute-done | bytes 5336 | tf_op jit(solution)/shard_map/ppermute | solution.py:334
  65.9 5.9 %collective-permute-start.7 = (f32[2,663]{1,0:T(2,128)S(1)}, f32[2,663]{1,0:T(2,128)S(1)}, u32[]{:S(2)}, u32[]{:S(2)}) collective-permute-start(f32[2,663]{1,0:T(2,128)S(1)} %add.29), channel_id=1, source_target_pairs={{32,64},{64,32},{96,128},{128,96},{160,192},{192,160},{224,0},{0,2... | collective-permute-start | bytes 15920 | tf_op jit(solution)/shard_map/ppermute | solution.py:334
  71.7 1.6 %collective-permute-done.7 = f32[2,663]{1,0:T(2,128)S(1)} collective-permute-done((f32[2,663]{1,0:T(2,128)S(1)}, f32[2,663]{1,0:T(2,128)S(1)}, u32[]{:S(2)}, u32[]{:S(2)}) %collective-permute-start.7) | collective-permute-done | bytes 5336 | tf_op jit(solution)/shard_map/ppermute | solution.py:334
  73.3 2.0 %collective-permute-start.8 = (f32[2,663]{1,0:T(2,128)S(1)}, f32[2,663]{1,0:T(2,128)S(1)}, u32[]{:S(2)}, u32[]{:S(2)}) collective-permute-start(f32[2,663]{1,0:T(2,128)S(1)} %add.30), channel_id=1, source_target_pairs={{64,160},{160,64},{32,192},{192,32},{0,96},{96,0},{128,224},{224,1... | collective-permute-start | bytes 15920 | tf_op jit(solution)/shard_map/ppermute | solution.py:334
  75.3 0.6 add_multiply_fusion
  76.0 2.8 %collective-permute-done.8 = f32[2,663]{1,0:T(2,128)S(1)} collective-permute-done((f32[2,663]{1,0:T(2,128)S(1)}, f32[2,663]{1,0:T(2,128)S(1)}, u32[]{:S(2)}, u32[]{:S(2)}) %collective-permute-start.8) | collective-permute-done | bytes 5336 | tf_op jit(solution)/shard_map/ppermute | solution.py:334
  78.8 0.6 add.31
  (25 shorter events, 0.1 us)
Async XLA Ops:
  0.6 5.4 %copy-start.6 = (s32[4,24,1326]{2,1,0:T(8,128)S(1)}, s32[4,24,1326]{2,1,0:T(8,128)}, u32[]{:S(2)}) copy-start(s32[4,24,1326]{2,1,0:T(8,128)} %param.13) | copy-start | bytes 1527556
  0.6 5.4 %copy-start.9 = (bf16[2,2,768,768]{3,2,1,0:T(8,128)(2,1)S(1)}, bf16[2,2,768,768]{3,2,1,0:T(8,128)(2,1)}, u32[]{:S(2)}) copy-start(bf16[2,2,768,768]{3,2,1,0:T(8,128)(2,1)} %constant.17.table_ref) | copy-start | bytes 14155780
  3.7 21.7 %collective-permute-start = (bf16[6,576,128]{2,1,0:T(8,128)(2,1)}, bf16[6,576,128]{2,1,0:T(8,128)(2,1)S(1)}, u32[]{:S(2)}, u32[]{:S(2)}) collective-permute-start(bf16[6,576,128]{2,1,0:T(8,128)(2,1)} %shard_map.129.ops_ref), channel_id=1, source_target_pairs={{0,1},{1,0},{2,3},{3,2},{4,5},{5,4},{6,7},{7,6},{8,9},{9,8},{10,11... | collective-permute-start | bytes 2654216 | tf_op jit(solution)/shard_map/ppermute | solution.py:334
  6.0 1.2 %copy-start.2 = (bf16[6,576,128]{2,1,0:T(8,128)(2,1)S(1)}, bf16[6,576,128]{2,1,0:T(8,128)(2,1)}, u32[]{:S(2)}) copy-start(bf16[6,576,128]{2,1,0:T(8,128)(2,1)} %shard_map.129.ops_ref) | copy-start | bytes 2654212
  7.2 18.1 %copy-start = (f32[4,24,4,663]{3,2,1,0:T(4,128)S(1)}, f32[4,24,4,663]{3,2,1,0:T(4,128)}, u32[]{:S(2)}) copy-start(f32[4,24,4,663]{3,2,1,0:T(4,128)} %param.17) | copy-start | bytes 3055108
  7.2 18.1 %copy-start.1 = (f32[4,24,3,663]{3,1,2,0:T(8,128)S(1)}, f32[4,24,3,663]{3,1,2,0:T(8,128)}, u32[]{:S(2)}) copy-start(f32[4,24,3,663]{3,1,2,0:T(8,128)} %param.16) | copy-start | bytes 2291332
  7.2 18.1 %copy-start.3 = (s32[2,2,768]{2,1,0:T(2,128)S(1)}, s32[2,2,768]{2,1,0:T(2,128)}, u32[]{:S(2)}) copy-start(s32[2,2,768]{2,1,0:T(2,128)} %constant.7.clone.refs_0_.refs_1_.refs_2_.cards_ref) | copy-start | bytes 36868
  7.2 18.1 %copy-start.4 = (s32[4,4]{1,0:T(4,128)S(1)}, s32[4,4]{1,0:T(4,128)}, u32[]{:S(2)}) copy-start(s32[4,4]{1,0:T(4,128)} %turn_ref.3) | copy-start | bytes 196
  7.2 18.1 %copy-start.5 = (s32[4,24]{1,0:T(4,128)S(1)}, s32[4,24]{1,0:T(4,128)}, u32[]{:S(2)}) copy-start(s32[4,24]{1,0:T(4,128)} %river_ref.3) | copy-start | bytes 1156
  7.2 18.1 %copy-start.7 = (s32[4,2]{0,1:T(2,128)S(1)}, s32[4,2]{0,1:T(2,128)}, u32[]{:S(2)}) copy-start(s32[4,2]{0,1:T(2,128)} %param.15) | copy-start | bytes 100
  7.3 18.1 %copy-start.8 = (s32[4]{0:T(128)S(1)}, s32[4]{0:T(128)}, u32[]{:S(2)}) copy-start(s32[4]{0:T(128)} %pot_ref.1) | copy-start | bytes 52
  47.3 1.3 %collective-permute-start.2 = (f32[2,663]{1,0:T(2,128)S(1)}, f32[2,663]{1,0:T(2,128)S(1)}, u32[]{:S(2)}, u32[]{:S(2)}) collective-permute-start(f32[2,663]{1,0:T(2,128)S(1)} %get-tuple-element.13), channel_id=1, source_target_pairs={{0,2},{2,0},{1,3},{3,1},{4,6},{6,4},{5,7},{7,5},{8,10},{10,8},{9,1... | collective-permute-start | bytes 15920 | tf_op jit(solution)/shard_map/ppermute | solution.py:334
  48.6 3.6 %collective-permute-start.3 = (f32[2,663]{1,0:T(2,128)S(1)}, f32[2,663]{1,0:T(2,128)S(1)}, u32[]{:S(2)}, u32[]{:S(2)}) collective-permute-start(f32[2,663]{1,0:T(2,128)S(1)} %add.25), channel_id=1, source_target_pairs={{0,4},{4,0},{8,12},{12,8},{1,5},{5,1},{9,13},{13,9},{2,6},{6,2},{1... | collective-permute-start | bytes 15920 | tf_op jit(solution)/shard_map/ppermute | solution.py:334
  52.2 4.8 %collective-permute-start.4 = (f32[2,663]{1,0:T(2,128)S(1)}, f32[2,663]{1,0:T(2,128)S(1)}, u32[]{:S(2)}, u32[]{:S(2)}) collective-permute-start(f32[2,663]{1,0:T(2,128)S(1)} %add.26), channel_id=1, source_target_pairs={{0,12},{12,0},{4,8},{8,4},{1,13},{13,1},{5,9},{9,5},{2,14},{14,2},... | collective-permute-start | bytes 15920 | tf_op jit(solution)/shard_map/ppermute | solution.py:334
  55.3 20.1 %collective-permute-start.1 = (f32[4,2,663]{2,1,0:T(2,128)S(1)}, f32[4,2,663]{2,1,0:T(2,128)S(1)}, u32[]{:S(2)}, u32[]{:S(2)}) collective-permute-start(f32[4,2,663]{2,1,0:T(2,128)S(1)} %get-tuple-element.12), channel_id=1, source_target_pairs={{0,2},{2,0},{1,3},{3,1},{4,6},{6,4},{5,7},{7,5},{8,10},{10,8},{9,1... | collective-permute-start | bytes 63656 | tf_op jit(solution)/shard_map/ppermute | solution.py:334
  57.1 5.1 %collective-permute-start.5 = (f32[2,663]{1,0:T(2,128)S(1)}, f32[2,663]{1,0:T(2,128)S(1)}, u32[]{:S(2)}, u32[]{:S(2)}) collective-permute-start(f32[2,663]{1,0:T(2,128)S(1)} %add.27), channel_id=1, source_target_pairs={{0,16},{16,0},{1,17},{17,1},{2,18},{18,2},{3,19},{19,3},{4,20},{20... | collective-permute-start | bytes 15920 | tf_op jit(solution)/shard_map/ppermute | solution.py:334
  62.2 3.6 %collective-permute-start.6 = (f32[2,663]{1,0:T(2,128)S(1)}, f32[2,663]{1,0:T(2,128)S(1)}, u32[]{:S(2)}, u32[]{:S(2)}) collective-permute-start(f32[2,663]{1,0:T(2,128)S(1)} %add.28), channel_id=1, source_target_pairs={{0,32},{32,0},{64,96},{96,64},{128,160},{160,128},{192,224},{224,1... | collective-permute-start | bytes 15920 | tf_op jit(solution)/shard_map/ppermute | solution.py:334
  65.9 7.5 %collective-permute-start.7 = (f32[2,663]{1,0:T(2,128)S(1)}, f32[2,663]{1,0:T(2,128)S(1)}, u32[]{:S(2)}, u32[]{:S(2)}) collective-permute-start(f32[2,663]{1,0:T(2,128)S(1)} %add.29), channel_id=1, source_target_pairs={{32,64},{64,32},{96,128},{128,96},{160,192},{192,160},{224,0},{0,2... | collective-permute-start | bytes 15920 | tf_op jit(solution)/shard_map/ppermute | solution.py:334
  73.3 5.4 %collective-permute-start.8 = (f32[2,663]{1,0:T(2,128)S(1)}, f32[2,663]{1,0:T(2,128)S(1)}, u32[]{:S(2)}, u32[]{:S(2)}) collective-permute-start(f32[2,663]{1,0:T(2,128)S(1)} %add.30), channel_id=1, source_target_pairs={{64,160},{160,64},{32,192},{192,32},{0,96},{96,0},{128,224},{224,1... | collective-permute-start | bytes 15920 | tf_op jit(solution)/shard_map/ppermute | solution.py:334

commit v3 on v2

--- a/solution.py
+++ b/solution.py
@@ -104,7 +104,7 @@
 
 
 def opposing_sums(slot, ranks_ref, ops_ref, table_ref, show_ref, contact_ref, scratch):
-    compat, negative, rows, staged, columns, rolled, wide, sem = scratch
+    compat, rows, staged, columns, rolled, wide, sem = scratch
     hand = lax.axis_index("hand")
     fetch = pltpu.make_async_copy(table_ref.at[hand, slot], compat, sem)
     fetch.start()
@@ -120,7 +120,6 @@
         wide[tile, : 6 * PAIRS, :] = ops_ref[tile].astype(jnp.float32)
         wide[tile, 6 * PAIRS :, :] = jnp.zeros((2 * PAIRS, 128), jnp.float32)
     fetch.wait()
-    negative[...] = -compat[...]
 
     chunk = 2 * PAIRS
     for m in range(3):
@@ -174,7 +173,7 @@
     opposing_sums(0, ranks_ref, ops_ref, table_ref, show_ref, contact_ref, scratch)
 
 
-def final_kernel(
+def values_kernel(
     turn_ref,
     pot_ref,
     bet_ref,
@@ -186,67 +185,44 @@
     *refs,
 ):
     sources = refs[:4]
-    values_ref, flop_ref, new_first_ref, new_second_ref = refs[4:8]
-    show_other, contact_other, staged_in, staged_out = refs[8:12]
-    held = refs[12:16]
-    sems = refs[16:20]
+    values_ref, flop_ref, show_other, contact_other, staged = refs[4:9]
+    held = refs[9:13]
+    sems = refs[13:17]
     copies = [pltpu.make_async_copy(*each) for each in zip(sources, held, sems)]
     for copy in copies:
         copy.start()
-    opposing_sums(1, ranks_ref, ops_ref, table_ref, show_other, contact_other, refs[20:])
+    opposing_sums(1, ranks_ref, ops_ref, table_ref, show_other, contact_other, refs[17:])
     for copy in copies:
         copy.wait()
     show_own, contact_own, first_ref, second_ref = held
     for tile in range(TILES):
         settle(
             tile,
-            turn_ref,
-            pot_ref,
-            bet_ref,
-            river_ref,
-            cards_ref,
-            first_ref,
-            second_ref,
-            staged_in,
-            staged_out,
-            show_own.at[tile],
-            show_other.at[tile],
-            contact_own.at[tile],
-            contact_other.at[tile],
-            values_ref,
-            flop_ref,
-            new_first_ref,
-            new_second_ref,
+            (turn_ref, pot_ref, bet_ref, river_ref, cards_ref, first_ref, second_ref),
+            (show_own, show_other, contact_own, contact_other),
+            staged,
+            (values_ref, flop_ref),
+            None,
         )
 
 
-def settle(
-    tile,
-    turn_ref,
-    pot_ref,
-    bet_ref,
-    river_ref,
-    cards_ref,
-    first_ref,
-    second_ref,
-    staged_in,
-    staged_out,
-    show_own,
-    show_other,
-    contact_own,
-    contact_other,
-    values_ref,
-    flop_ref,
-    new_first_ref,
-    new_second_ref,
-):
+def regrets_kernel(*refs):
+    for tile in range(TILES):
+        settle(tile, refs[:7], refs[7:11], refs[13], None, (refs[11], refs[12], refs[14]))
+
+
+def settle(tile, inputs, sums, staged_in, values, regrets):
+    turn_ref, pot_ref, bet_ref, river_ref, cards_ref, first_ref, second_ref = inputs
+    show_own, show_other, contact_own, contact_other = [ref.at[tile] for ref in sums]
     hand = lax.axis_index("hand")
     width = min(128, HALF - tile * 128)
     lanes = slice(tile * 128, tile * 128 + width)
     wide_lanes = slice(tile * 128, (tile + 1) * 128)
     staged_in[:, :, :width] = second_ref[:, :, lanes]
     flat = staged_in.reshape(PAIRS * 4, 128)
-    new_flat = staged_out.reshape(PAIRS * 4, 128)
+    if regrets is not None:
+        new_first_ref, new_second_ref, staged_out = regrets
+        new_flat = staged_out.reshape(PAIRS * 4, 128)
     for turn in range(TURNS_HERE):
         alive = alive_rows(cards_ref.at[:, :, wide_lanes], turn_ref, river_ref, hand, turn)
         alive = alive.astype(jnp.float32)
@@ -273,12 +249,11 @@
         utility = [value[:, :width] for value in utility]
         total = actions[0] + actions[1] + actions[2]
         v1 = (
-            actions[0] / total * utility[0]
-            + actions[1] / total * utility[1]
-            + actions[2] / total * utility[2]
-        )
-        for a in range(3):
-            new_first_ref[turn, a, :, lanes] = jnp.maximum(actions[a] + utility[a] - v1, 0.0)
+            actions[0] * utility[0] + actions[1] * utility[1] + actions[2] * utility[2]
+        ) / total
+        if regrets is not None:
+            for a in range(3):
+                new_first_ref[turn, a, :, lanes] = jnp.maximum(actions[a] + utility[a] - v1, 0.0)
         v2 = 0.5 * show(3) * alive
         for b in range(2):
             fold, call = second_rows(flat, turn, b)
@@ -287,6 +262,8 @@
             call_value = share[b] * show(4 + b) * alive
             node = (1.0 - prob) * fold_value + prob * call_value
             v2 = v2 + node
+            if regrets is None:
+                continue
             row = turn * RIVERS_HERE * 4 + 2 * b
             new_flat[pl.ds(row, RIVERS_HERE, stride=4), :] = jnp.maximum(
                 fold + fold_value - node, 0.0
@@ -294,13 +271,17 @@
             new_flat[pl.ds(row + 1, RIVERS_HERE, stride=4), :] = jnp.maximum(
                 call + call_value - node, 0.0
             )
-        sums = (jnp.sum(v1, axis=0, keepdims=True), jnp.sum(v2, axis=0, keepdims=True)[:, :width])
+        if values is None:
+            continue
+        values_ref, flop_ref = values
+        summed = (jnp.sum(v1, axis=0, keepdims=True), jnp.sum(v2, axis=0, keepdims=True)[:, :width])
         for player in range(2):
-            values_ref[turn, player : player + 1, lanes] = sums[player]
-        totals = sums if turn == 0 else [total + each for total, each in zip(totals, sums)]
-    for player in range(2):
+            values_ref[turn, player : player + 1, lanes] = summed[player]
+        totals = summed if turn == 0 else [total + each for total, each in zip(totals, summed)]
+    for player in range(2 if values is not None else 0):
         flop_ref[player : player + 1, lanes] = totals[player] * (1.0 / RIVERS)
-    new_second_ref[:, :, lanes] = staged_out[:, :, :width]
+    if regrets is not None:
+        new_second_ref[:, :, lanes] = staged_out[:, :, :width]
 
 
 def whole(space=pltpu.VMEM):
@@ -320,7 +301,6 @@
 def sum_scratch():
     return [
         pltpu.VMEM((WIDTH, WIDTH), jnp.bfloat16),
-        pltpu.VMEM((WIDTH, WIDTH), jnp.bfloat16),
         pltpu.VMEM((PAIRS, WIDTH), jnp.float32),
         pltpu.VMEM((128, WIDTH), jnp.float32),
         pltpu.VMEM((WIDTH, 128), jnp.float32),
@@ -332,6 +312,22 @@
 
 def exchange(value, axis, *pairs):
     return lax.ppermute(value, axis, [p for a, b in pairs for p in ((a, b), (b, a))])
+
+
+def depth_sum(value):
+    def routes(first, second):
+        return [
+            pair
+            for i in range(8)
+            for pair in (((i + first) % 8 * 2, i * 2), ((i + second) % 8 * 2 + 1, i * 2 + 1))
+        ]
+
+    axes = ("z", "river")
+    near = lax.ppermute(value, axes, routes(-1, 1))
+    three = value + near + exchange(near, "river", (0, 1))
+    sent = jnp.where(lax.axis_index("river") == 0, three, value + near)
+    far = lax.ppermute(sent, axes, routes(3, -3))
+    return three + far + exchange(far, "river", (0, 1))
 
 
 def shards(
@@ -393,20 +389,18 @@
         cost_estimate=sums_cost,
     )(ranks, operands, table)
 
-    partial, flop_values, new_first, new_second = pl.pallas_call(
-        final_kernel,
+    bets = bet_chips.T
+    partial, flop_values, show_other, contact_other = pl.pallas_call(
+        values_kernel,
         out_shape=(
             jax.ShapeDtypeStruct((TURNS_HERE, 2, HALF), jnp.float32),
             jax.ShapeDtypeStruct((2, HALF), jnp.float32),
-            jax.ShapeDtypeStruct(first.shape, jnp.float32),
-            jax.ShapeDtypeStruct(second.shape, jnp.float32),
+            jax.ShapeDtypeStruct(show_shape, jnp.float32),
+            jax.ShapeDtypeStruct(contact_shape, jnp.float32),
         ),
         in_specs=[whole(pltpu.SMEM)] * 3 + [whole()] * 4 + [whole(pl.ANY)] * 5,
-        out_specs=(whole(), whole(), whole(), whole()),
+        out_specs=(whole(),) * 4,
         scratch_shapes=[
-            pltpu.VMEM(show_shape, jnp.float32),
-            pltpu.VMEM(contact_shape, jnp.float32),
-            pltpu.VMEM((PAIRS, 4, 128), jnp.float32),
             pltpu.VMEM((PAIRS, 4, 128), jnp.float32),
             pltpu.VMEM(show_shape, jnp.float32),
             pltpu.VMEM(contact_shape, jnp.float32),
@@ -420,7 +414,7 @@
     )(
         turn_cards,
         pot_chips,
-        bet_chips.T,
+        bets,
         river_cards,
         cards,
         ranks,
@@ -431,15 +425,37 @@
         first,
         second,
     )
-
+    new_first, new_second = pl.pallas_call(
+        regrets_kernel,
+        out_shape=(
+            jax.ShapeDtypeStruct(first.shape, jnp.float32),
+            jax.ShapeDtypeStruct(second.shape, jnp.float32),
+        ),
+        in_specs=[whole(pltpu.SMEM)] * 3 + [whole()] * 8,
+        out_specs=(whole(), whole()),
+        scratch_shapes=[pltpu.VMEM((PAIRS, 4, 128), jnp.float32)] * 2,
+        compiler_params=params,
+        cost_estimate=pl.CostEstimate(flops=1 << 23, bytes_accessed=1 << 23, transcendentals=0),
+    )(
+        turn_cards,
+        pot_chips,
+        bets,
+        river_cards,
+        cards,
+        first,
+        second,
+        show,
+        show_other,
+        contact,
+        contact_other,
+    )
+
+    flop_values = flop_values + exchange(flop_values, "river", (0, 1))
+    flop_values = depth_sum(flop_values)
     for axis, pairs in (
-        ("river", ((0, 1),)),
         ("y", ((0, 1), (2, 3))),
         ("y", ((0, 3), (1, 2))),
         ("xh", ((0, 1),)),
-        ("z", ((0, 1), (2, 3), (4, 5), (6, 7))),
-        ("z", ((1, 2), (3, 4), (5, 6), (7, 0))),
-        ("z", ((2, 5), (1, 6), (0, 3), (4, 7))),
     ):
         flop_values = flop_values + exchange(flop_values, axis, *pairs)
     turn_values = (partial + exchange(partial, "river", (0, 1))) / RIVERS

time: 79.5 us -> 87.9 us (1.11)
  local copies, waits for them, and re-layouts: 1.24 us -> 12.6 us
  starting transfers between devices: 18.9 us -> 13.1 us
  Pallas kernels: 42.5 us -> 44 us
    unnamed x20 -> x36, local copies, waits for them, and re-layouts: 1.24 us -> 12.6 us
    ppermute x9 -> x8, starting transfers between devices: 18.9 us -> 9.97 us  [exchange(): lax.ppermute(value, axis, [p for a, b in pairs for p in ((a, b), (b, a))])]
    ppermute x0 -> x2, waiting for transfers between devices: none -> 8.06 us  [the longest x1 5.54 us: depth_sum(): near = lax.ppermute(value, axes, routes(-1, 1))]
    ppermute x9 -> x8, waiting for transfers between devices: 14.7 us -> 7.13 us  [exchange(): lax.ppermute(value, axis, [p for a, b in pairs for p in ((a, b), (b, a))])]
    ppermute x0 -> x2, starting transfers between devices: none -> 3.17 us  [the longest x1 2.99 us: depth_sum(): far = lax.ppermute(sent, axes, routes(3, -3))]
    pallas_call x1 -> x2, Pallas kernels: 21.9 us -> 23.5 us  [the longest x1 20.4 us: shards(): pl.pallas_call(values_kernel, out_shape=(jax.ShapeDtypeStruct((TURNS_HERE...]
  transfers between devices with their start and end apart: 9 -> 10, of which waited for: 8 -> 7; matrix products, arithmetic and copies ran while one was open for 1% -> 1% of each run, Pallas kernels for 22% -> 24%
where the time goes in v3:
time: 87.9 us; the launch traced here: 86.9 us
  Pallas kernels  44 us (50%)
  waiting for transfers between devices  15.2 us (17%)
  starting transfers between devices  13.1 us (15%)
  local copies, waits for them, and re-layouts  12.6 us (14%)
  other arithmetic  1.25 us (1%)
    pallas_call x1, Pallas kernels, shards(): pl.pallas_call(values_kernel, out_shape=(jax.ShapeDtypeStruct((TURNS_HERE...  20.4 us
    pallas_call x1, Pallas kernels, shards(): pl.pallas_call(own_kernel, out_shape=(jax.ShapeDtypeStruct(show_shape, jn...  17.6 us
    unnamed x36, local copies, waits for them, and re-layouts  12.6 us
    ppermute x8, starting transfers between devices, exchange(): lax.ppermute(value, axis, [p for a, b in pairs for p in ((a, b), (b, a))])  9.97 us
    ppermute x8, waiting for transfers between devices, exchange(): lax.ppermute(value, axis, [p for a, b in pairs for p in ((a, b), (b, a))])  7.13 us
    ppermute x1, waiting for transfers between devices, depth_sum(): near = lax.ppermute(value, axes, routes(-1, 1))  5.54 us
    pallas_call x1, Pallas kernels, shards(): pl.pallas_call(regrets_kernel, out_shape=(jax.ShapeDtypeStruct(first.shap...  3.15 us
    ppermute x1, starting transfers between devices, depth_sum(): far = lax.ppermute(sent, axes, routes(3, -3))  2.99 us
  transfers between devices with their start and end apart: 10, of which 7 were waited for; matrix products, arithmetic and copies ran while one was open for 1% of the time, Pallas kernels for 24%

profile of v3, /device:TPU:2, one launch (start us, length us, event | category | flops | bytes accessed | tf_op | source)
XLA Modules:
  0.0 86.9 jit_solution(83407437463316101)
XLA Ops:
  0.6 2.9 %shard_map.129.ops_ref = bf16[6,576,128]{2,1,0:T(8,128)(2,1)} custom-call(s32[4,4]{1,0:T(4,128)} %refs_0_.2, s32[4,24]{1,0:T(4,128)} %refs_3_.3, s32[2,2,768]{2,1,0:T(2,128)} %constant.13.clone.refs_0_.refs_1_.refs_2_.cards_ref.refs_4_, s32[2,2,768]{2,1,0:T(2,128)} %constant.13.clone.refs_0_.refs_1_.refs_2_.cards_ref.refs_4_, ...), custom_call_target="tpu_custom_call" | custom-call | flops 4194304 | bytes 4194304 | tf_op jit(solution)/shard_map/pallas_call | solution.py:357
  3.5 2.4 %collective-permute-start = (bf16[6,576,128]{2,1,0:T(8,128)(2,1)}, bf16[6,576,128]{2,1,0:T(8,128)(2,1)S(1)}, u32[]{:S(2)}, u32[]{:S(2)}) collective-permute-start(bf16[6,576,128]{2,1,0:T(8,128)(2,1)} %shard_map.129.ops_ref), channel_id=1, source_target_pairs={{0,1},{1,0},{2,3},{3,2},{4,5},{5,4},{6,7},{7,6},{8,9},{9,8},{10,11... | collective-permute-start | bytes 2654216 | tf_op jit(solution)/shard_map/ppermute | solution.py:314
  5.9 1.2 %copy-done.10 = bf16[6,576,128]{2,1,0:T(8,128)(2,1)S(1)} copy-done((bf16[6,576,128]{2,1,0:T(8,128)(2,1)S(1)}, bf16[6,576,128]{2,1,0:T(8,128)(2,1)}, u32[]{:S(2)}) %copy-start.10) | copy-done | bytes 884760
  7.1 2.3 %copy-done.17 = bf16[2,2,768,768]{3,2,1,0:T(8,128)(2,1)S(1)} copy-done((bf16[2,2,768,768]{3,2,1,0:T(8,128)(2,1)S(1)}, bf16[2,2,768,768]{3,2,1,0:T(8,128)(2,1)}, u32[]{:S(2)}) %copy-start.17) | copy-done | bytes 4718616
  9.5 17.6 %shard_map.130 = (f32[6,768,128]{2,1,0:T(8,128)S(1)}, f32[6,576,128]{2,1,0:T(8,128)S(1)}) custom-call(s32[96,1326]{1,0:T(8,128)S(1)} %bitcast.18, bf16[6,576,128]{2,1,0:T(8,128)(2,1)S(1)} %copy-done.10, bf16[2,2,768,768]{3,2,1,0:T(8,128)(2,1)S(1)} %copy-done.17), custom_call_target="tpu_custom_call" | custom-call | flops 25367150592 | bytes 8388608 | tf_op jit(solution)/shard_map/pallas_call | solution.py:379
  27.1 20.4 %shard_map.131 = (f32[4,2,663]{2,1,0:T(2,128)S(1)}, f32[2,663]{1,0:T(2,128)S(1)}, f32[6,768,128]{2,1,0:T(8,128)S(1)}, f32[6,576,128]{2,1,0:T(8,128)S(1)}) custom-call(s32[4,4]{1,0:T(4,128)S(1)} %copy-done.12, s32[4]{0:T(128)S(1)} %copy-done.15, s32[2,4]{1,0:T(2,128)S(1)} %bitcast.16, s32[4,24]{1,0:T(4,128)S(1)} %copy-done.13, s32[2,2,768]{2,1,0:T(2,128)S(1)} %copy-done.11, ...), custom_call_target="tpu_custom_call" | custom-call | flops 25367150592 | bytes 8388608 | tf_op jit(solution)/shard_map/pallas_call | solution.py:393
  47.5 1.4 %copy-done.4 = f32[6,768,128]{2,1,0:T(8,128)} copy-done((f32[6,768,128]{2,1,0:T(8,128)}, f32[6,768,128]{2,1,0:T(8,128)S(1)}, u32[]{:S(2)}) %copy-start.4) | copy-done | bytes 2359320
  49.0 1.3 %copy-done.8 = f32[6,576,128]{2,1,0:T(8,128)} copy-done((f32[6,576,128]{2,1,0:T(8,128)}, f32[6,576,128]{2,1,0:T(8,128)S(1)}, u32[]{:S(2)}) %copy-start.8) | copy-done | bytes 1769496
  50.3 1.2 %collective-permute-done.2 = f32[2,663]{1,0:T(2,128)S(1)} collective-permute-done((f32[2,663]{1,0:T(2,128)S(1)}, f32[2,663]{1,0:T(2,128)S(1)}, u32[]{:S(2)}, u32[]{:S(2)}) %collective-permute-start.2) | collective-permute-done | bytes 5336 | tf_op jit(solution)/shard_map/ppermute | solution.py:314
  51.6 5.5 %collective-permute-done.3 = f32[2,663]{1,0:T(2,128)S(1)} collective-permute-done((f32[2,663]{1,0:T(2,128)S(1)}, f32[2,663]{1,0:T(2,128)S(1)}, u32[]{:S(2)}, u32[]{:S(2)}) %collective-permute-start.3) | collective-permute-done | bytes 5336 | tf_op jit(solution)/shard_map/ppermute | solution.py:326
  57.2 1.2 %collective-permute-done.4 = f32[2,663]{1,0:T(2,128)S(1)} collective-permute-done((f32[2,663]{1,0:T(2,128)S(1)}, f32[2,663]{1,0:T(2,128)S(1)}, u32[]{:S(2)}, u32[]{:S(2)}) %collective-permute-start.4) | collective-permute-done | bytes 5336 | tf_op jit(solution)/shard_map/ppermute | solution.py:314
  58.4 3.0 %collective-permute-start.5 = (f32[2,663]{1,0:T(2,128)S(1)}, f32[2,663]{1,0:T(2,128)S(1)}, u32[]{:S(2)}, u32[]{:S(2)}) collective-permute-start(f32[2,663]{1,0:T(2,128)S(1)} %get-tuple-element.20), channel_id=1, source_target_pairs={{96,0},{162,2},{128,32},{194,34},{160,64},{226,66},{192,96},{2,98}... | collective-permute-start | bytes 15920 | tf_op jit(solution)/shard_map/ppermute | solution.py:329
  61.3 2.5 %collective-permute-done.5 = f32[2,663]{1,0:T(2,128)S(1)} collective-permute-done((f32[2,663]{1,0:T(2,128)S(1)}, f32[2,663]{1,0:T(2,128)S(1)}, u32[]{:S(2)}, u32[]{:S(2)}) %collective-permute-start.5) | collective-permute-done | bytes 5336 | tf_op jit(solution)/shard_map/ppermute | solution.py:329
  64.4 0.7 collective-permute-done.6
  65.0 1.6 %collective-permute-start.7 = (f32[2,663]{1,0:T(2,128)S(1)}, f32[2,663]{1,0:T(2,128)S(1)}, u32[]{:S(2)}, u32[]{:S(2)}) collective-permute-start(f32[2,663]{1,0:T(2,128)S(1)} %add_add_fusion), channel_id=1, source_target_pairs={{0,4},{4,0},{8,12},{12,8},{1,5},{5,1},{9,13},{13,9},{2,6},{6,2},{1... | collective-permute-start | bytes 15920 | tf_op jit(solution)/shard_map/ppermute | solution.py:314
  66.6 2.1 %collective-permute-done.7 = f32[2,663]{1,0:T(2,128)S(1)} collective-permute-done((f32[2,663]{1,0:T(2,128)S(1)}, f32[2,663]{1,0:T(2,128)S(1)}, u32[]{:S(2)}, u32[]{:S(2)}) %collective-permute-start.7) | collective-permute-done | bytes 5336 | tf_op jit(solution)/shard_map/ppermute | solution.py:314
  68.7 3.0 %collective-permute-start.8 = (f32[2,663]{1,0:T(2,128)S(1)}, f32[2,663]{1,0:T(2,128)S(1)}, u32[]{:S(2)}, u32[]{:S(2)}) collective-permute-start(f32[2,663]{1,0:T(2,128)S(1)} %add.34), channel_id=1, source_target_pairs={{0,12},{12,0},{4,8},{8,4},{1,13},{13,1},{5,9},{9,5},{2,14},{14,2},... | collective-permute-start | bytes 15920 | tf_op jit(solution)/shard_map/ppermute | solution.py:314
  71.7 1.7 %copy-done.3 = f32[6,768,128]{2,1,0:T(8,128)S(1)} copy-done((f32[6,768,128]{2,1,0:T(8,128)S(1)}, f32[6,768,128]{2,1,0:T(8,128)}, u32[]{:S(2)}) %copy-start.3) | copy-done | bytes 2359320
  73.4 1.7 %copy-done.5 = f32[6,768,128]{2,1,0:T(8,128)S(1)} copy-done((f32[6,768,128]{2,1,0:T(8,128)S(1)}, f32[6,768,128]{2,1,0:T(8,128)}, u32[]{:S(2)}) %copy-start.5) | copy-done | bytes 2359320
  75.0 1.5 %copy-done.7 = f32[6,576,128]{2,1,0:T(8,128)S(1)} copy-done((f32[6,576,128]{2,1,0:T(8,128)S(1)}, f32[6,576,128]{2,1,0:T(8,128)}, u32[]{:S(2)}) %copy-start.7) | copy-done | bytes 1769496
  76.5 1.5 %copy-done.9 = f32[6,576,128]{2,1,0:T(8,128)S(1)} copy-done((f32[6,576,128]{2,1,0:T(8,128)S(1)}, f32[6,576,128]{2,1,0:T(8,128)}, u32[]{:S(2)}) %copy-start.9) | copy-done | bytes 1769496
  78.0 3.1 %shard_map.132 = (f32[4,3,24,663]{3,2,1,0:T(8,128)}, f32[96,4,663]{2,1,0:T(4,128)}) custom-call(s32[4,4]{1,0:T(4,128)S(1)} %copy-done.12, s32[4]{0:T(128)S(1)} %copy-done.15, s32[2,4]{1,0:T(2,128)S(1)} %bitcast.17, s32[4,24]{1,0:T(4,128)S(1)} %copy-done.13, s32[2,2,768]{2,1,0:T(2,128)S(1)} %copy-done.11, f32[4,3,24,663]{3,2,1,0:T(8,128)S(1)} %bitcast.15, ...), custom_call_target="tpu_custom_call" | custom-call | flops 8388608 | bytes 8388608 | tf_op jit(solution)/shard_map/pallas_call | solution.py:428
  81.1 2.5 %collective-permute-start.9 = (f32[2,663]{1,0:T(2,128)S(1)}, f32[2,663]{1,0:T(2,128)S(1)}, u32[]{:S(2)}, u32[]{:S(2)}) collective-permute-start(f32[2,663]{1,0:T(2,128)S(1)} %add.35), channel_id=1, source_target_pairs={{0,16},{16,0},{1,17},{17,1},{2,18},{18,2},{3,19},{19,3},{4,20},{20... | collective-permute-start | bytes 15920 | tf_op jit(solution)/shard_map/ppermute | solution.py:314
  84.3 2.1 %collective-permute-done.9 = f32[2,663]{1,0:T(2,128)S(1)} collective-permute-done((f32[2,663]{1,0:T(2,128)S(1)}, f32[2,663]{1,0:T(2,128)S(1)}, u32[]{:S(2)}, u32[]{:S(2)}) %collective-permute-start.9) | collective-permute-done | bytes 5336 | tf_op jit(solution)/shard_map/ppermute | solution.py:314
  (43 shorter events, 2.0 us)
Async XLA Ops:
  0.6 5.3 %copy-start.16 = (s32[4,24,1326]{2,1,0:T(8,128)S(1)}, s32[4,24,1326]{2,1,0:T(8,128)}, u32[]{:S(2)}) copy-start(s32[4,24,1326]{2,1,0:T(8,128)} %param.13) | copy-start | bytes 1527556
  3.5 23.5 %collective-permute-start = (bf16[6,576,128]{2,1,0:T(8,128)(2,1)}, bf16[6,576,128]{2,1,0:T(8,128)(2,1)S(1)}, u32[]{:S(2)}, u32[]{:S(2)}) collective-permute-start(bf16[6,576,128]{2,1,0:T(8,128)(2,1)} %shard_map.129.ops_ref), channel_id=1, source_target_pairs={{0,1},{1,0},{2,3},{3,2},{4,5},{5,4},{6,7},{7,6},{8,9},{9,8},{10,11... | collective-permute-start | bytes 2654216 | tf_op jit(solution)/shard_map/ppermute | solution.py:314
  7.1 2.3 %copy-start.17 = (bf16[2,2,768,768]{3,2,1,0:T(8,128)(2,1)S(1)}, bf16[2,2,768,768]{3,2,1,0:T(8,128)(2,1)}, u32[]{:S(2)}) copy-start(bf16[2,2,768,768]{3,2,1,0:T(8,128)(2,1)} %constant.23.table_ref) | copy-start | bytes 14155780
  9.4 17.6 %copy-start = (f32[4,24,4,663]{3,2,1,0:T(4,128)S(1)}, f32[4,24,4,663]{3,2,1,0:T(4,128)}, u32[]{:S(2)}) copy-start(f32[4,24,4,663]{3,2,1,0:T(4,128)} %param.17) | copy-start | bytes 3055108
  9.4 17.7 %copy-start.1 = (f32[4,24,3,663]{3,1,2,0:T(8,128)S(1)}, f32[4,24,3,663]{3,1,2,0:T(8,128)}, u32[]{:S(2)}) copy-start(f32[4,24,3,663]{3,1,2,0:T(8,128)} %param.16) | copy-start | bytes 2291332
  9.4 17.7 %copy-start.11 = (s32[2,2,768]{2,1,0:T(2,128)S(1)}, s32[2,2,768]{2,1,0:T(2,128)}, u32[]{:S(2)}) copy-start(s32[2,2,768]{2,1,0:T(2,128)} %constant.13.clone.refs_0_.refs_1_.refs_2_.cards_ref.refs_4_) | copy-start | bytes 36868
  9.4 17.7 %copy-start.12 = (s32[4,4]{1,0:T(4,128)S(1)}, s32[4,4]{1,0:T(4,128)}, u32[]{:S(2)}) copy-start(s32[4,4]{1,0:T(4,128)} %refs_0_.2) | copy-start | bytes 196
  9.4 17.7 %copy-start.13 = (s32[4,24]{1,0:T(4,128)S(1)}, s32[4,24]{1,0:T(4,128)}, u32[]{:S(2)}) copy-start(s32[4,24]{1,0:T(4,128)} %refs_3_.3) | copy-start | bytes 1156
  9.4 17.7 %copy-start.14 = (s32[4,2]{0,1:T(2,128)S(1)}, s32[4,2]{0,1:T(2,128)}, u32[]{:S(2)}) copy-start(s32[4,2]{0,1:T(2,128)} %param.15) | copy-start | bytes 100
  9.5 17.7 %copy-start.15 = (s32[4]{0:T(128)S(1)}, s32[4]{0:T(128)}, u32[]{:S(2)}) copy-start(s32[4]{0:T(128)} %refs_1_.2) | copy-start | bytes 52
  27.0 20.5 %copy-start.2 = (f32[6,768,128]{2,1,0:T(8,128)}, f32[6,768,128]{2,1,0:T(8,128)S(1)}, u32[]{:S(2)}) copy-start(f32[6,768,128]{2,1,0:T(8,128)S(1)} %get-tuple-element.12.refs_0_.refs_7_) | copy-start | bytes 7077892
  27.0 20.5 %copy-start.6 = (f32[6,576,128]{2,1,0:T(8,128)}, f32[6,576,128]{2,1,0:T(8,128)S(1)}, u32[]{:S(2)}) copy-start(f32[6,576,128]{2,1,0:T(8,128)S(1)} %get-tuple-element.13.refs_1_.refs_9_) | copy-start | bytes 5308420
  50.3 1.2 %collective-permute-start.2 = (f32[2,663]{1,0:T(2,128)S(1)}, f32[2,663]{1,0:T(2,128)S(1)}, u32[]{:S(2)}, u32[]{:S(2)}) collective-permute-start(f32[2,663]{1,0:T(2,128)S(1)} %get-tuple-element.15), channel_id=1, source_target_pairs={{0,2},{2,0},{1,3},{3,1},{4,6},{6,4},{5,7},{7,5},{8,10},{10,8},{9,1... | collective-permute-start | bytes 15920 | tf_op jit(solution)/shard_map/ppermute | solution.py:314
  51.4 5.7 %collective-permute-start.3 = (f32[2,663]{1,0:T(2,128)S(1)}, f32[2,663]{1,0:T(2,128)S(1)}, u32[]{:S(2)}, u32[]{:S(2)}) collective-permute-start(f32[2,663]{1,0:T(2,128)S(1)} %add.29), channel_id=1, source_target_pairs={{224,0},{34,2},{0,32},{66,34},{32,64},{98,66},{64,96},{130,98},{96... | collective-permute-start | bytes 15920 | tf_op jit(solution)/shard_map/ppermute | solution.py:326
  57.2 1.2 %collective-permute-start.4 = (f32[2,663]{1,0:T(2,128)S(1)}, f32[2,663]{1,0:T(2,128)S(1)}, u32[]{:S(2)}, u32[]{:S(2)}) collective-permute-start(f32[2,663]{1,0:T(2,128)S(1)} %collective-permute-done.3), channel_id=1, source_target_pairs={{0,2},{2,0},{1,3},{3,1},{4,6},{6,4},{5,7},{7,5},{8,10},{10,8},{9,1... | collective-permute-start | bytes 15920 | tf_op jit(solution)/shard_map/ppermute | solution.py:314
  58.4 5.5 %collective-permute-start.5 = (f32[2,663]{1,0:T(2,128)S(1)}, f32[2,663]{1,0:T(2,128)S(1)}, u32[]{:S(2)}, u32[]{:S(2)}) collective-permute-start(f32[2,663]{1,0:T(2,128)S(1)} %get-tuple-element.20), channel_id=1, source_target_pairs={{96,0},{162,2},{128,32},{194,34},{160,64},{226,66},{192,96},{2,98}... | collective-permute-start | bytes 15920 | tf_op jit(solution)/shard_map/ppermute | solution.py:329
  63.9 1.2 %collective-permute-start.6 = (f32[2,663]{1,0:T(2,128)S(1)}, f32[2,663]{1,0:T(2,128)S(1)}, u32[]{:S(2)}, u32[]{:S(2)}) collective-permute-start(f32[2,663]{1,0:T(2,128)S(1)} %collective-permute-done.5), channel_id=1, source_target_pairs={{0,2},{2,0},{1,3},{3,1},{4,6},{6,4},{5,7},{7,5},{8,10},{10,8},{9,1... | collective-permute-start | bytes 15920 | tf_op jit(solution)/shard_map/ppermute | solution.py:314
  64.0 19.6 %collective-permute-start.1 = (f32[4,2,663]{2,1,0:T(2,128)S(1)}, f32[4,2,663]{2,1,0:T(2,128)S(1)}, u32[]{:S(2)}, u32[]{:S(2)}) collective-permute-start(f32[4,2,663]{2,1,0:T(2,128)S(1)} %get-tuple-element.14), channel_id=1, source_target_pairs={{0,2},{2,0},{1,3},{3,1},{4,6},{6,4},{5,7},{7,5},{8,10},{10,8},{9,1... | collective-permute-start | bytes 63656 | tf_op jit(solution)/shard_map/ppermute | solution.py:314
  65.0 3.6 %collective-permute-start.7 = (f32[2,663]{1,0:T(2,128)S(1)}, f32[2,663]{1,0:T(2,128)S(1)}, u32[]{:S(2)}, u32[]{:S(2)}) collective-permute-start(f32[2,663]{1,0:T(2,128)S(1)} %add_add_fusion), channel_id=1, source_target_pairs={{0,4},{4,0},{8,12},{12,8},{1,5},{5,1},{9,13},{13,9},{2,6},{6,2},{1... | collective-permute-start | bytes 15920 | tf_op jit(solution)/shard_map/ppermute | solution.py:314
  68.7 12.5 %collective-permute-start.8 = (f32[2,663]{1,0:T(2,128)S(1)}, f32[2,663]{1,0:T(2,128)S(1)}, u32[]{:S(2)}, u32[]{:S(2)}) collective-permute-start(f32[2,663]{1,0:T(2,128)S(1)} %add.34), channel_id=1, source_target_pairs={{0,12},{12,0},{4,8},{8,4},{1,13},{13,1},{5,9},{9,5},{2,14},{14,2},... | collective-permute-start | bytes 15920 | tf_op jit(solution)/shard_map/ppermute | solution.py:314
  71.7 1.7 %copy-start.3 = (f32[6,768,128]{2,1,0:T(8,128)S(1)}, f32[6,768,128]{2,1,0:T(8,128)}, u32[]{:S(2)}) copy-start(f32[6,768,128]{2,1,0:T(8,128)} %copy-done.2) | copy-start | bytes 7077892
  73.4 1.7 %copy-start.5 = (f32[6,768,128]{2,1,0:T(8,128)S(1)}, f32[6,768,128]{2,1,0:T(8,128)}, u32[]{:S(2)}) copy-start(f32[6,768,128]{2,1,0:T(8,128)} %copy-done.4) | copy-start | bytes 7077892
  75.0 1.5 %copy-start.7 = (f32[6,576,128]{2,1,0:T(8,128)S(1)}, f32[6,576,128]{2,1,0:T(8,128)}, u32[]{:S(2)}) copy-start(f32[6,576,128]{2,1,0:T(8,128)} %copy-done.6) | copy-start | bytes 5308420
  81.1 5.2 %collective-permute-start.9 = (f32[2,663]{1,0:T(2,128)S(1)}, f32[2,663]{1,0:T(2,128)S(1)}, u32[]{:S(2)}, u32[]{:S(2)}) collective-permute-start(f32[2,663]{1,0:T(2,128)S(1)} %add.35), channel_id=1, source_target_pairs={{0,16},{16,0},{1,17},{17,1},{2,18},{18,2},{3,19},{19,3},{4,20},{20... | collective-permute-start | bytes 15920 | tf_op jit(solution)/shard_map/ppermute | solution.py:314
  (4 other events, 5.4 us)

commit v4 on v3

--- a/solution.py
+++ b/solution.py
@@ -43,23 +43,24 @@
     return halves, compat
 
 
-def alive_rows(cards_ref, turn_ref, river_ref, hand, turn):
+def river_column(river_ref, turn):
+    row = jnp.broadcast_to(river_ref[pl.ds(turn, 1), :], (RIVERS_HERE, RIVERS_HERE))
+    diagonal = lax.broadcasted_iota(jnp.int32, row.shape, 0) == lax.broadcasted_iota(
+        jnp.int32, row.shape, 1
+    )
+    column = jnp.sum(jnp.where(diagonal, row, 0), axis=1, keepdims=True)
+    return jnp.broadcast_to(column, (RIVERS_HERE, 128))
+
+
+def alive_rows(cards_ref, turn_ref, column, hand, turn):
     low = jnp.where(hand == 0, cards_ref[0, 0:1, :], cards_ref[1, 0:1, :])
     high = jnp.where(hand == 0, cards_ref[0, 1:2, :], cards_ref[1, 1:2, :])
-    good = low >= 0
     for k in range(4):
         dead = turn_ref[turn, k]
-        good = good & (low != dead) & (high != dead)
-    row = jnp.broadcast_to(river_ref[turn : turn + 1, :], (RIVERS_HERE, RIVERS_HERE))
-    diagonal = lax.broadcasted_iota(jnp.int32, row.shape, 0) == lax.broadcasted_iota(
-        jnp.int32, row.shape, 1
-    )
-    column = jnp.sum(jnp.where(diagonal, row, 0), axis=1, keepdims=True)
-    column = jnp.broadcast_to(column, (RIVERS_HERE, 128))
+        low = jnp.where((low == dead) | (high == dead), -1, low)
     low = jnp.broadcast_to(low, column.shape)
     high = jnp.broadcast_to(high, column.shape)
-    good = jnp.broadcast_to(good.astype(jnp.int32), column.shape)
-    return (good > 0) & (low != column) & (high != column)
+    return (low >= 0) & (low != column) & (high != column)
 
 
 def second_rows(flat, turn, b):
@@ -73,13 +74,14 @@
     hand = lax.axis_index("hand")
     scaling = 2.0 / HANDS
     out_ref = refs[-1]
+    columns = [river_column(river_ref, turn) for turn in range(TURNS_HERE)]
     for tile in range(STEP_TILES):
         cards_ref, reach_ref, first_ref, second_ref = refs[tile:-1:STEP_TILES]
         flat = second_ref.reshape(PAIRS * 4, 128)
         for two in range(TURNS_HERE // 2):
             parts = []
             for turn in (2 * two, 2 * two + 1):
-                alive = alive_rows(cards_ref, turn_ref, river_ref, hand, turn)
+                alive = alive_rows(cards_ref, turn_ref, columns[turn], hand, turn)
                 x = jnp.where(alive, reach_ref[turn, 0:1, :] * scaling, 0.0)
                 y = jnp.where(alive, reach_ref[turn, 1:2, :] * scaling, 0.0)
                 actions = [first_ref[turn, a] for a in range(3)]
@@ -103,7 +105,7 @@
     )
 
 
-def opposing_sums(slot, ranks_ref, ops_ref, table_ref, show_ref, contact_ref, scratch):
+def opposing_sums(slot, unroll, ranks_ref, ops_ref, table_ref, contact_ref, scratch, put, before, after):
     compat, rows, staged, columns, rolled, wide, sem = scratch
     hand = lax.axis_index("hand")
     fetch = pltpu.make_async_copy(table_ref.at[hand, slot], compat, sem)
@@ -140,9 +142,10 @@
                 ]
 
     def group(g, carry):
-        rolled[...] = pltpu.roll(columns[...], 128 - g * UNROLL, 1)
-        for j in range(UNROLL):
-            pair = g * UNROLL + j
+        before(g)
+        rolled[...] = pltpu.roll(columns[...], 128 - g * unroll, 1)
+        for j in range(unroll):
+            pair = g * unroll + j
             picked = pl.ds(pair, 8, stride=PAIRS)
             left = jnp.concatenate([wide[tile, picked, :] for tile in range(TILES)], axis=1)
             left = left.astype(jnp.bfloat16)
@@ -163,125 +166,129 @@
                     )
             for n in range(3):
                 for i in range(2):
-                    show_ref[2 * n + i, picked, :] = accs[n][:, i * 128 : (i + 1) * 128]
+                    put(g, j, 2 * n + i, accs[n][:, i * 128 : (i + 1) * 128])
+        after(g)
         return carry
 
-    lax.fori_loop(0, PAIRS // UNROLL, group, 0)
+    lax.fori_loop(0, PAIRS // unroll, group, 0)
 
 
 def own_kernel(ranks_ref, ops_ref, table_ref, show_ref, contact_ref, *scratch):
-    opposing_sums(0, ranks_ref, ops_ref, table_ref, show_ref, contact_ref, scratch)
-
-
-def values_kernel(
-    turn_ref,
-    pot_ref,
-    bet_ref,
-    river_ref,
-    cards_ref,
-    ranks_ref,
-    ops_ref,
-    table_ref,
-    *refs,
-):
-    sources = refs[:4]
-    values_ref, flop_ref, show_other, contact_other, staged = refs[4:9]
-    held = refs[9:13]
-    sems = refs[13:17]
-    copies = [pltpu.make_async_copy(*each) for each in zip(sources, held, sems)]
-    for copy in copies:
-        copy.start()
-    opposing_sums(1, ranks_ref, ops_ref, table_ref, show_other, contact_other, refs[17:])
-    for copy in copies:
-        copy.wait()
-    show_own, contact_own, first_ref, second_ref = held
-    for tile in range(TILES):
-        settle(
-            tile,
-            (turn_ref, pot_ref, bet_ref, river_ref, cards_ref, first_ref, second_ref),
-            (show_own, show_other, contact_own, contact_other),
-            staged,
-            (values_ref, flop_ref),
-            None,
-        )
-
-
-def regrets_kernel(*refs):
-    for tile in range(TILES):
-        settle(tile, refs[:7], refs[7:11], refs[13], None, (refs[11], refs[12], refs[14]))
-
-
-def settle(tile, inputs, sums, staged_in, values, regrets):
-    turn_ref, pot_ref, bet_ref, river_ref, cards_ref, first_ref, second_ref = inputs
-    show_own, show_other, contact_own, contact_other = [ref.at[tile] for ref in sums]
-    hand = lax.axis_index("hand")
-    width = min(128, HALF - tile * 128)
-    lanes = slice(tile * 128, tile * 128 + width)
-    wide_lanes = slice(tile * 128, (tile + 1) * 128)
-    staged_in[:, :, :width] = second_ref[:, :, lanes]
-    flat = staged_in.reshape(PAIRS * 4, 128)
-    if regrets is not None:
-        new_first_ref, new_second_ref, staged_out = regrets
-        new_flat = staged_out.reshape(PAIRS * 4, 128)
-    for turn in range(TURNS_HERE):
-        alive = alive_rows(cards_ref.at[:, :, wide_lanes], turn_ref, river_ref, hand, turn)
-        alive = alive.astype(jnp.float32)
+    def put(g, j, tile, value):
+        show_ref[tile, pl.ds(g * UNROLL + j, 8, stride=PAIRS), :] = value
+
+    def nothing(g):
+        pass
+
+    opposing_sums(
+        0, UNROLL, ranks_ref, ops_ref, table_ref, contact_ref, scratch, put, nothing, nothing
+    )
+
+
+def final_kernel(*refs):
+    inputs = refs[:5] + refs[8:10]
+    ranks_ref, ops_ref, table_ref, show_own, contact_own = refs[5:8] + refs[10:12]
+    values_ref, flop_ref, new_first_ref, new_second_ref = refs[12:16]
+    fresh, ready, contact_other, staged_in, staged_out = refs[16:21]
+    sums = (show_own, ready, contact_own, contact_other)
+    ready[...] = jnp.zeros_like(ready)
+
+    turn_ref, pot_ref, bet_ref, river_ref = inputs[:4]
+
+    def settle_turn(turn):
+        column = river_column(river_ref, turn)
         pot = jnp.full((1, 128), pot_ref[turn], jnp.int32).astype(jnp.float32)
         share = [
             0.5 + jnp.full((1, 128), bet_ref[b, turn], jnp.int32).astype(jnp.float32) / pot
             for b in range(2)
         ]
-
-        def rows_of(own, other, c):
-            start = c * PAIRS + turn * RIVERS_HERE
-            here = slice(start, start + RIVERS_HERE)
-            return own[here, :] + other[here, :]
-
-        show = functools.partial(rows_of, show_own, show_other)
-        contact = functools.partial(rows_of, contact_own, contact_other)
-        base = contact(0)
-        utility = [
-            0.5 * show(0) * alive,
-            (0.5 * (base - contact(1)) + share[0] * show(1)) * alive,
-            (0.5 * (base - contact(2)) + share[1] * show(2)) * alive,
-        ]
-        actions = [first_ref[turn, a, :, lanes] for a in range(3)]
-        utility = [value[:, :width] for value in utility]
-        total = actions[0] + actions[1] + actions[2]
-        v1 = (
-            actions[0] * utility[0] + actions[1] * utility[1] + actions[2] * utility[2]
-        ) / total
-        if regrets is not None:
-            for a in range(3):
-                new_first_ref[turn, a, :, lanes] = jnp.maximum(actions[a] + utility[a] - v1, 0.0)
-        v2 = 0.5 * show(3) * alive
-        for b in range(2):
-            fold, call = second_rows(flat, turn, b)
-            prob = call / (fold + call)
-            fold_value = -0.5 * contact(4 + b) * alive
-            call_value = share[b] * show(4 + b) * alive
-            node = (1.0 - prob) * fold_value + prob * call_value
-            v2 = v2 + node
-            if regrets is None:
-                continue
-            row = turn * RIVERS_HERE * 4 + 2 * b
-            new_flat[pl.ds(row, RIVERS_HERE, stride=4), :] = jnp.maximum(
-                fold + fold_value - node, 0.0
+        for tile in range(TILES):
+            settle(
+                tile,
+                turn,
+                column,
+                share,
+                (turn_ref,) + inputs[4:],
+                sums,
+                (staged_in.at[tile], staged_out.at[tile]),
+                (values_ref, new_first_ref, new_second_ref),
             )
-            new_flat[pl.ds(row + 1, RIVERS_HERE, stride=4), :] = jnp.maximum(
-                call + call_value - node, 0.0
-            )
-        if values is None:
-            continue
-        values_ref, flop_ref = values
-        summed = (jnp.sum(v1, axis=0, keepdims=True), jnp.sum(v2, axis=0, keepdims=True)[:, :width])
-        for player in range(2):
-            values_ref[turn, player : player + 1, lanes] = summed[player]
-        totals = summed if turn == 0 else [total + each for total, each in zip(totals, summed)]
-    for player in range(2 if values is not None else 0):
-        flop_ref[player : player + 1, lanes] = totals[player] * (1.0 / RIVERS)
-    if regrets is not None:
-        new_second_ref[:, :, lanes] = staged_out[:, :, :width]
+
+    def put(g, j, tile, value):
+        fresh[tile, pl.ds(j, 8, stride=RIVERS_HERE), :] = value
+
+    def before(g):
+        settle_turn(jnp.maximum(g - 1, 0))
+
+    def after(g):
+        ready[...] = fresh[...]
+
+    opposing_sums(
+        1, RIVERS_HERE, ranks_ref, ops_ref, table_ref, contact_other, refs[21:], put, before, after
+    )
+    settle_turn(TURNS_HERE - 1)
+    total = values_ref[0]
+    for turn in range(1, TURNS_HERE):
+        total = total + values_ref[turn]
+    flop_ref[...] = total * (1.0 / RIVERS)
+
+
+def settle(tile, turn, column, share, inputs, sums, staged, outputs):
+    turn_ref, cards_ref, first_ref, second_ref = inputs
+    show_own, show_other, contact_own, contact_other = [ref.at[tile] for ref in sums]
+    staged_in, staged_out = staged
+    values_ref, new_first_ref, new_second_ref = outputs
+    hand = lax.axis_index("hand")
+    width = min(128, HALF - tile * 128)
+    lanes = slice(tile * 128, tile * 128 + width)
+    wide_lanes = slice(tile * 128, (tile + 1) * 128)
+    rivers = pl.ds(turn * RIVERS_HERE, RIVERS_HERE)
+    staged_in[:, :, :width] = second_ref[rivers, :, lanes]
+    flat = staged_in.reshape(RIVERS_HERE * 4, 128)
+    new_flat = staged_out.reshape(RIVERS_HERE * 4, 128)
+    alive = alive_rows(cards_ref.at[:, :, wide_lanes], turn_ref, column, hand, turn)
+    alive = alive.astype(jnp.float32)
+
+    def rows_of(ref, c):
+        start = c * PAIRS + turn * RIVERS_HERE
+        return ref[pl.ds(pl.multiple_of(start, 8), RIVERS_HERE), :]
+
+    def show(c):
+        return rows_of(show_own, c) + show_other[c * RIVERS_HERE : (c + 1) * RIVERS_HERE, :]
+
+    def contact(c):
+        return rows_of(contact_own, c) + rows_of(contact_other, c)
+
+    base = contact(0)
+    utility = [
+        0.5 * show(0) * alive,
+        (0.5 * (base - contact(1)) + share[0] * show(1)) * alive,
+        (0.5 * (base - contact(2)) + share[1] * show(2)) * alive,
+    ]
+    actions = [first_ref[turn, a, :, lanes] for a in range(3)]
+    utility = [value[:, :width] for value in utility]
+    total = actions[0] + actions[1] + actions[2]
+    v1 = (actions[0] * utility[0] + actions[1] * utility[1] + actions[2] * utility[2]) / total
+    for a in range(3):
+        new_first_ref[turn, a, :, lanes] = jnp.maximum(actions[a] + utility[a] - v1, 0.0)
+    v2 = 0.5 * show(3) * alive
+    for b in range(2):
+        fold, call = second_rows(flat, 0, b)
+        prob = call / (fold + call)
+        fold_value = -0.5 * contact(4 + b) * alive
+        call_value = share[b] * show(4 + b) * alive
+        node = (1.0 - prob) * fold_value + prob * call_value
+        v2 = v2 + node
+        new_flat[pl.ds(2 * b, RIVERS_HERE, stride=4), :] = jnp.maximum(
+            fold + fold_value - node, 0.0
+        )
+        new_flat[pl.ds(2 * b + 1, RIVERS_HERE, stride=4), :] = jnp.maximum(
+            call + call_value - node, 0.0
+        )
+    new_second_ref[rivers, :, lanes] = staged_out[:, :, :width]
+    summed = (jnp.sum(v1, axis=0, keepdims=True), jnp.sum(v2, axis=0, keepdims=True)[:, :width])
+    for player in range(2):
+        values_ref[turn, player : player + 1, lanes] = summed[player]
 
 
 def whole(space=pltpu.VMEM):
@@ -390,24 +397,25 @@
     )(ranks, operands, table)
 
     bets = bet_chips.T
-    partial, flop_values, show_other, contact_other = pl.pallas_call(
-        values_kernel,
+    fresh_shape = (TILES, 8 * RIVERS_HERE, 128)
+    staged_shape = (TILES, RIVERS_HERE, 4, 128)
+    partial, flop_values, new_first, new_second = pl.pallas_call(
+        final_kernel,
         out_shape=(
             jax.ShapeDtypeStruct((TURNS_HERE, 2, HALF), jnp.float32),
             jax.ShapeDtypeStruct((2, HALF), jnp.float32),
-            jax.ShapeDtypeStruct(show_shape, jnp.float32),
-            jax.ShapeDtypeStruct(contact_shape, jnp.float32),
+            jax.ShapeDtypeStruct(first.shape, jnp.float32),
+            jax.ShapeDtypeStruct(second.shape, jnp.float32),
         ),
-        in_specs=[whole(pltpu.SMEM)] * 3 + [whole()] * 4 + [whole(pl.ANY)] * 5,
+        in_specs=[whole(pltpu.SMEM)] * 3 + [whole()] * 4 + [whole(pl.ANY)] + [whole()] * 4,
         out_specs=(whole(),) * 4,
         scratch_shapes=[
-            pltpu.VMEM((PAIRS, 4, 128), jnp.float32),
-            pltpu.VMEM(show_shape, jnp.float32),
+            pltpu.VMEM(fresh_shape, jnp.float32),
+            pltpu.VMEM(fresh_shape, jnp.float32),
             pltpu.VMEM(contact_shape, jnp.float32),
-            pltpu.VMEM(first.shape, jnp.float32),
-            pltpu.VMEM(second.shape, jnp.float32),
+            pltpu.VMEM(staged_shape, jnp.float32),
+            pltpu.VMEM(staged_shape, jnp.float32),
         ]
-        + [pltpu.SemaphoreType.DMA] * 4
         + sum_scratch(),
         compiler_params=params,
         cost_estimate=sums_cost,
@@ -420,36 +428,11 @@
         ranks,
         others,
         table,
-        show,
-        contact,
-        first,
-        second,
-    )
-    new_first, new_second = pl.pallas_call(
-        regrets_kernel,
-        out_shape=(
-            jax.ShapeDtypeStruct(first.shape, jnp.float32),
-            jax.ShapeDtypeStruct(second.shape, jnp.float32),
-        ),
-        in_specs=[whole(pltpu.SMEM)] * 3 + [whole()] * 8,
-        out_specs=(whole(), whole()),
-        scratch_shapes=[pltpu.VMEM((PAIRS, 4, 128), jnp.float32)] * 2,
-        compiler_params=params,
-        cost_estimate=pl.CostEstimate(flops=1 << 23, bytes_accessed=1 << 23, transcendentals=0),
-    )(
-        turn_cards,
-        pot_chips,
-        bets,
-        river_cards,
-        cards,
         first,
         second,
         show,
-        show_other,
         contact,
-        contact_other,
-    )
-
+    )
     flop_values = flop_values + exchange(flop_values, "river", (0, 1))
     flop_values = depth_sum(flop_values)
     for axis, pairs in (

time: 87.9 us -> 76.9 us (0.87)
  local copies, waits for them, and re-layouts: 12.6 us -> 1.25 us
  Pallas kernels: 44 us -> 41 us
  waiting for transfers between devices: 15.2 us -> 17.8 us
  starting transfers between devices: 13.1 us -> 14.8 us
    unnamed x36 -> x22, local copies, waits for them, and re-layouts: 12.6 us -> 1.25 us
    pallas_call x2 -> x1, Pallas kernels: 23.5 us -> 20.5 us  [shards(): pl.pallas_call(final_kernel, out_shape=(jax.ShapeDtypeStruct((TURNS_HERE,...]
    ppermute x8, waiting for transfers between devices: 7.13 us -> 9.74 us  [exchange(): lax.ppermute(value, axis, [p for a, b in pairs for p in ((a, b), (b, a))])]
    ppermute x1, starting transfers between devices: 0.18 us -> 1.91 us  [depth_sum(): near = lax.ppermute(value, axes, routes(-1, 1))]
  transfers between devices with their start and end apart: 10 -> 10, of which waited for: 7 -> 9; matrix products, arithmetic and copies ran while one was open for 1% -> 1% of each run, Pallas kernels for 24% -> 23%
where the time goes in v4:
time: 76.9 us; the launch traced here: 76.8 us
  Pallas kernels  41 us (53%)
  waiting for transfers between devices  17.8 us (23%)
  starting transfers between devices  14.8 us (19%)
  local copies, waits for them, and re-layouts  1.25 us (2%)
  other arithmetic  1.25 us (2%)
  between operations  0.77 us (1%)
    pallas_call x1, Pallas kernels, shards(): pl.pallas_call(final_kernel, out_shape=(jax.ShapeDtypeStruct((TURNS_HERE,...  20.5 us
    pallas_call x1, Pallas kernels, shards(): pl.pallas_call(own_kernel, out_shape=(jax.ShapeDtypeStruct(show_shape, jn...  17.6 us
    ppermute x8, starting transfers between devices, exchange(): lax.ppermute(value, axis, [p for a, b in pairs for p in ((a, b), (b, a))])  9.86 us
    ppermute x8, waiting for transfers between devices, exchange(): lax.ppermute(value, axis, [p for a, b in pairs for p in ((a, b), (b, a))])  9.74 us
    ppermute x1, waiting for transfers between devices, depth_sum(): near = lax.ppermute(value, axes, routes(-1, 1))  5.54 us
    ppermute x1, starting transfers between devices, depth_sum(): far = lax.ppermute(sent, axes, routes(3, -3))  2.99 us
    pallas_call x1, Pallas kernels, shards(): pl.pallas_call(operand_kernel, grid=(TILES // STEP_TILES,), out_shape=jax...  2.97 us
    ppermute x1, waiting for transfers between devices, depth_sum(): far = lax.ppermute(sent, axes, routes(3, -3))  2.51 us
  transfers between devices with their start and end apart: 10, of which 9 were waited for; matrix products, arithmetic and copies ran while one was open for 1% of the time, Pallas kernels for 23%

profile of v4, /device:TPU:2, one launch (start us, length us, event | category | flops | bytes accessed | tf_op | source)
XLA Modules:
  0.0 76.8 jit_solution(1605176290961902455)
XLA Ops:
  0.7 3.0 %shard_map.129.ops_ref = bf16[6,576,128]{2,1,0:T(8,128)(2,1)} custom-call(s32[4,4]{1,0:T(4,128)} %refs_0_.2, s32[4,24]{1,0:T(4,128)} %refs_3_.3, s32[2,2,768]{2,1,0:T(2,128)} %constant.13.clone.refs_0_.refs_1_.refs_2_.refs_4_, s32[2,2,768]{2,1,0:T(2,128)} %constant.13.clone.refs_0_.refs_1_.refs_2_.refs_4_, ...), custom_call_target="tpu_custom_call" | custom-call | flops 4194304 | bytes 4194304 | tf_op jit(solution)/shard_map/pallas_call | solution.py:364
  3.6 2.4 %collective-permute-start = (bf16[6,576,128]{2,1,0:T(8,128)(2,1)}, bf16[6,576,128]{2,1,0:T(8,128)(2,1)S(1)}, u32[]{:S(2)}, u32[]{:S(2)}) collective-permute-start(bf16[6,576,128]{2,1,0:T(8,128)(2,1)} %shard_map.129.ops_ref), channel_id=1, source_target_pairs={{0,1},{1,0},{2,3},{3,2},{4,5},{5,4},{6,7},{7,6},{8,9},{9,8},{10,11... | collective-permute-start | bytes 2654216 | tf_op jit(solution)/shard_map/ppermute | solution.py:321
  6.0 1.2 %copy-done.2 = bf16[6,576,128]{2,1,0:T(8,128)(2,1)S(1)} copy-done((bf16[6,576,128]{2,1,0:T(8,128)(2,1)S(1)}, bf16[6,576,128]{2,1,0:T(8,128)(2,1)}, u32[]{:S(2)}) %copy-start.2) | copy-done | bytes 884760
  7.2 17.6 %shard_map.130 = (f32[6,768,128]{2,1,0:T(8,128)S(1)}, f32[6,576,128]{2,1,0:T(8,128)S(1)}) custom-call(s32[96,1326]{1,0:T(8,128)S(1)} %bitcast.14, bf16[6,576,128]{2,1,0:T(8,128)(2,1)S(1)} %copy-done.2, bf16[2,2,768,768]{3,2,1,0:T(8,128)(2,1)S(1)} %copy-done.9), custom_call_target="tpu_custom_call" | custom-call | flops 25367150592 | bytes 8388608 | tf_op jit(solution)/shard_map/pallas_call | solution.py:386
  24.8 0.5 collective-permute-done.refs_6_
  25.4 20.5 %shard_map.131 = (f32[4,2,663]{2,1,0:T(2,128)S(1)}, f32[2,663]{1,0:T(2,128)S(1)}, f32[4,3,24,663]{3,2,1,0:T(8,128)}, f32[96,4,663]{2,1,0:T(4,128)}) custom-call(s32[4,4]{1,0:T(4,128)S(1)} %copy-done.4, s32[4]{0:T(128)S(1)} %copy-done.8, s32[2,4]{1,0:T(2,128)S(1)} %bitcast.16, s32[4,24]{1,0:T(4,128)S(1)} %copy-done.5, s32[2,2,768]{2,1,0:T(2,128)S(1)} %copy-done.3, ...), custom_call_target="tpu_custom_call" | custom-call | flops 25367150592 | bytes 8388608 | tf_op jit(solution)/shard_map/pallas_call | solution.py:402
  45.8 0.3 collective-permute-start.2
  46.1 1.2 %collective-permute-done.2 = f32[2,663]{1,0:T(2,128)S(1)} collective-permute-done((f32[2,663]{1,0:T(2,128)S(1)}, f32[2,663]{1,0:T(2,128)S(1)}, u32[]{:S(2)}, u32[]{:S(2)}) %collective-permute-start.2) | collective-permute-done | bytes 5336 | tf_op jit(solution)/shard_map/ppermute | solution.py:321
  47.3 1.9 %collective-permute-start.3 = (f32[2,663]{1,0:T(2,128)S(1)}, f32[2,663]{1,0:T(2,128)S(1)}, u32[]{:S(2)}, u32[]{:S(2)}) collective-permute-start(f32[2,663]{1,0:T(2,128)S(1)} %add.29), channel_id=1, source_target_pairs={{224,0},{34,2},{0,32},{66,34},{32,64},{98,66},{64,96},{130,98},{96... | collective-permute-start | bytes 15920 | tf_op jit(solution)/shard_map/ppermute | solution.py:333
  49.2 5.5 %collective-permute-done.3 = f32[2,663]{1,0:T(2,128)S(1)} collective-permute-done((f32[2,663]{1,0:T(2,128)S(1)}, f32[2,663]{1,0:T(2,128)S(1)}, u32[]{:S(2)}, u32[]{:S(2)}) %collective-permute-start.3) | collective-permute-done | bytes 5336 | tf_op jit(solution)/shard_map/ppermute | solution.py:333
  54.7 1.2 %collective-permute-done.4 = f32[2,663]{1,0:T(2,128)S(1)} collective-permute-done((f32[2,663]{1,0:T(2,128)S(1)}, f32[2,663]{1,0:T(2,128)S(1)}, u32[]{:S(2)}, u32[]{:S(2)}) %collective-permute-start.4) | collective-permute-done | bytes 5336 | tf_op jit(solution)/shard_map/ppermute | solution.py:321
  55.9 3.0 %collective-permute-start.5 = (f32[2,663]{1,0:T(2,128)S(1)}, f32[2,663]{1,0:T(2,128)S(1)}, u32[]{:S(2)}, u32[]{:S(2)}) collective-permute-start(f32[2,663]{1,0:T(2,128)S(1)} %get-tuple-element.16), channel_id=1, source_target_pairs={{96,0},{162,2},{128,32},{194,34},{160,64},{226,66},{192,96},{2,98}... | collective-permute-start | bytes 15920 | tf_op jit(solution)/shard_map/ppermute | solution.py:336
  58.9 2.5 %collective-permute-done.5 = f32[2,663]{1,0:T(2,128)S(1)} collective-permute-done((f32[2,663]{1,0:T(2,128)S(1)}, f32[2,663]{1,0:T(2,128)S(1)}, u32[]{:S(2)}, u32[]{:S(2)}) %collective-permute-start.5) | collective-permute-done | bytes 5336 | tf_op jit(solution)/shard_map/ppermute | solution.py:336
  61.4 0.2 collective-permute-start.6
  61.6 0.3 collective-permute-start.1
  61.9 0.7 collective-permute-done.6
  62.6 1.6 %collective-permute-start.7 = (f32[2,663]{1,0:T(2,128)S(1)}, f32[2,663]{1,0:T(2,128)S(1)}, u32[]{:S(2)}, u32[]{:S(2)}) collective-permute-start(f32[2,663]{1,0:T(2,128)S(1)} %add_add_fusion), channel_id=1, source_target_pairs={{0,4},{4,0},{8,12},{12,8},{1,5},{5,1},{9,13},{13,9},{2,6},{6,2},{1... | collective-permute-start | bytes 15920 | tf_op jit(solution)/shard_map/ppermute | solution.py:321
  64.2 2.1 %collective-permute-done.7 = f32[2,663]{1,0:T(2,128)S(1)} collective-permute-done((f32[2,663]{1,0:T(2,128)S(1)}, f32[2,663]{1,0:T(2,128)S(1)}, u32[]{:S(2)}, u32[]{:S(2)}) %collective-permute-start.7) | collective-permute-done | bytes 5336 | tf_op jit(solution)/shard_map/ppermute | solution.py:321
  66.2 3.0 %collective-permute-start.8 = (f32[2,663]{1,0:T(2,128)S(1)}, f32[2,663]{1,0:T(2,128)S(1)}, u32[]{:S(2)}, u32[]{:S(2)}) collective-permute-start(f32[2,663]{1,0:T(2,128)S(1)} %add.34), channel_id=1, source_target_pairs={{0,12},{12,0},{4,8},{8,4},{1,13},{13,1},{5,9},{9,5},{2,14},{14,2},... | collective-permute-start | bytes 15920 | tf_op jit(solution)/shard_map/ppermute | solution.py:321
  69.3 1.8 %collective-permute-done.8 = f32[2,663]{1,0:T(2,128)S(1)} collective-permute-done((f32[2,663]{1,0:T(2,128)S(1)}, f32[2,663]{1,0:T(2,128)S(1)}, u32[]{:S(2)}, u32[]{:S(2)}) %collective-permute-start.8) | collective-permute-done | bytes 5336 | tf_op jit(solution)/shard_map/ppermute | solution.py:321
  71.1 2.1 %collective-permute-start.9 = (f32[2,663]{1,0:T(2,128)S(1)}, f32[2,663]{1,0:T(2,128)S(1)}, u32[]{:S(2)}, u32[]{:S(2)}) collective-permute-start(f32[2,663]{1,0:T(2,128)S(1)} %add.35), channel_id=1, source_target_pairs={{0,16},{16,0},{1,17},{17,1},{2,18},{18,2},{3,19},{19,3},{4,20},{20... | collective-permute-start | bytes 15920 | tf_op jit(solution)/shard_map/ppermute | solution.py:321
  73.2 0.6 add_multiply_fusion
  73.8 2.4 %collective-permute-done.9 = f32[2,663]{1,0:T(2,128)S(1)} collective-permute-done((f32[2,663]{1,0:T(2,128)S(1)}, f32[2,663]{1,0:T(2,128)S(1)}, u32[]{:S(2)}, u32[]{:S(2)}) %collective-permute-start.9) | collective-permute-done | bytes 5336 | tf_op jit(solution)/shard_map/ppermute | solution.py:321
  76.2 0.6 add.36
  (28 shorter events, 0.1 us)
Async XLA Ops:
  0.6 5.4 %copy-start.6 = (s32[4,24,1326]{2,1,0:T(8,128)S(1)}, s32[4,24,1326]{2,1,0:T(8,128)}, u32[]{:S(2)}) copy-start(s32[4,24,1326]{2,1,0:T(8,128)} %param.13) | copy-start | bytes 1527556
  0.6 5.4 %copy-start.9 = (bf16[2,2,768,768]{3,2,1,0:T(8,128)(2,1)S(1)}, bf16[2,2,768,768]{3,2,1,0:T(8,128)(2,1)}, u32[]{:S(2)}) copy-start(bf16[2,2,768,768]{3,2,1,0:T(8,128)(2,1)} %constant.23.table_ref.refs_7_) | copy-start | bytes 14155780
  3.6 21.7 %collective-permute-start = (bf16[6,576,128]{2,1,0:T(8,128)(2,1)}, bf16[6,576,128]{2,1,0:T(8,128)(2,1)S(1)}, u32[]{:S(2)}, u32[]{:S(2)}) collective-permute-start(bf16[6,576,128]{2,1,0:T(8,128)(2,1)} %shard_map.129.ops_ref), channel_id=1, source_target_pairs={{0,1},{1,0},{2,3},{3,2},{4,5},{5,4},{6,7},{7,6},{8,9},{9,8},{10,11... | collective-permute-start | bytes 2654216 | tf_op jit(solution)/shard_map/ppermute | solution.py:321
  6.0 1.2 %copy-start.2 = (bf16[6,576,128]{2,1,0:T(8,128)(2,1)S(1)}, bf16[6,576,128]{2,1,0:T(8,128)(2,1)}, u32[]{:S(2)}) copy-start(bf16[6,576,128]{2,1,0:T(8,128)(2,1)} %shard_map.129.ops_ref) | copy-start | bytes 2654212
  7.2 18.1 %copy-start = (f32[4,24,4,663]{3,2,1,0:T(4,128)S(1)}, f32[4,24,4,663]{3,2,1,0:T(4,128)}, u32[]{:S(2)}) copy-start(f32[4,24,4,663]{3,2,1,0:T(4,128)} %param.17) | copy-start | bytes 3055108
  7.2 18.1 %copy-start.1 = (f32[4,24,3,663]{3,1,2,0:T(8,128)S(1)}, f32[4,24,3,663]{3,1,2,0:T(8,128)}, u32[]{:S(2)}) copy-start(f32[4,24,3,663]{3,1,2,0:T(8,128)} %param.16) | copy-start | bytes 2291332
  7.2 18.1 %copy-start.3 = (s32[2,2,768]{2,1,0:T(2,128)S(1)}, s32[2,2,768]{2,1,0:T(2,128)}, u32[]{:S(2)}) copy-start(s32[2,2,768]{2,1,0:T(2,128)} %constant.13.clone.refs_0_.refs_1_.refs_2_.refs_4_) | copy-start | bytes 36868
  7.2 18.1 %copy-start.4 = (s32[4,4]{1,0:T(4,128)S(1)}, s32[4,4]{1,0:T(4,128)}, u32[]{:S(2)}) copy-start(s32[4,4]{1,0:T(4,128)} %refs_0_.2) | copy-start | bytes 196
  7.2 18.1 %copy-start.5 = (s32[4,24]{1,0:T(4,128)S(1)}, s32[4,24]{1,0:T(4,128)}, u32[]{:S(2)}) copy-start(s32[4,24]{1,0:T(4,128)} %refs_3_.3) | copy-start | bytes 1156
  7.2 18.1 %copy-start.7 = (s32[4,2]{0,1:T(2,128)S(1)}, s32[4,2]{0,1:T(2,128)}, u32[]{:S(2)}) copy-start(s32[4,2]{0,1:T(2,128)} %param.15) | copy-start | bytes 100
  7.2 18.1 %copy-start.8 = (s32[4]{0:T(128)S(1)}, s32[4]{0:T(128)}, u32[]{:S(2)}) copy-start(s32[4]{0:T(128)} %refs_1_.2) | copy-start | bytes 52
  7.2 18.1 %copy-start.10 = (bf16[2,2,768,768]{3,2,1,0:T(8,128)(2,1)S(1)}, bf16[2,2,768,768]{3,2,1,0:T(8,128)(2,1)}, u32[]{:S(2)}) copy-start(bf16[2,2,768,768]{3,2,1,0:T(8,128)(2,1)} %constant.23.table_ref.refs_7_) | copy-start | bytes 14155780
  45.8 1.4 %collective-permute-start.2 = (f32[2,663]{1,0:T(2,128)S(1)}, f32[2,663]{1,0:T(2,128)S(1)}, u32[]{:S(2)}, u32[]{:S(2)}) collective-permute-start(f32[2,663]{1,0:T(2,128)S(1)} %get-tuple-element.13), channel_id=1, source_target_pairs={{0,2},{2,0},{1,3},{3,1},{4,6},{6,4},{5,7},{7,5},{8,10},{10,8},{9,1... | collective-permute-start | bytes 15920 | tf_op jit(solution)/shard_map/ppermute | solution.py:321
  47.3 7.5 %collective-permute-start.3 = (f32[2,663]{1,0:T(2,128)S(1)}, f32[2,663]{1,0:T(2,128)S(1)}, u32[]{:S(2)}, u32[]{:S(2)}) collective-permute-start(f32[2,663]{1,0:T(2,128)S(1)} %add.29), channel_id=1, source_target_pairs={{224,0},{34,2},{0,32},{66,34},{32,64},{98,66},{64,96},{130,98},{96... | collective-permute-start | bytes 15920 | tf_op jit(solution)/shard_map/ppermute | solution.py:333
  54.7 1.2 %collective-permute-start.4 = (f32[2,663]{1,0:T(2,128)S(1)}, f32[2,663]{1,0:T(2,128)S(1)}, u32[]{:S(2)}, u32[]{:S(2)}) collective-permute-start(f32[2,663]{1,0:T(2,128)S(1)} %collective-permute-done.3), channel_id=1, source_target_pairs={{0,2},{2,0},{1,3},{3,1},{4,6},{6,4},{5,7},{7,5},{8,10},{10,8},{9,1... | collective-permute-start | bytes 15920 | tf_op jit(solution)/shard_map/ppermute | solution.py:321
  55.9 5.5 %collective-permute-start.5 = (f32[2,663]{1,0:T(2,128)S(1)}, f32[2,663]{1,0:T(2,128)S(1)}, u32[]{:S(2)}, u32[]{:S(2)}) collective-permute-start(f32[2,663]{1,0:T(2,128)S(1)} %get-tuple-element.16), channel_id=1, source_target_pairs={{96,0},{162,2},{128,32},{194,34},{160,64},{226,66},{192,96},{2,98}... | collective-permute-start | bytes 15920 | tf_op jit(solution)/shard_map/ppermute | solution.py:336
  61.4 1.2 %collective-permute-start.6 = (f32[2,663]{1,0:T(2,128)S(1)}, f32[2,663]{1,0:T(2,128)S(1)}, u32[]{:S(2)}, u32[]{:S(2)}) collective-permute-start(f32[2,663]{1,0:T(2,128)S(1)} %collective-permute-done.5), channel_id=1, source_target_pairs={{0,2},{2,0},{1,3},{3,1},{4,6},{6,4},{5,7},{7,5},{8,10},{10,8},{9,1... | collective-permute-start | bytes 15920 | tf_op jit(solution)/shard_map/ppermute | solution.py:321
  61.6 11.6 %collective-permute-start.1 = (f32[4,2,663]{2,1,0:T(2,128)S(1)}, f32[4,2,663]{2,1,0:T(2,128)S(1)}, u32[]{:S(2)}, u32[]{:S(2)}) collective-permute-start(f32[4,2,663]{2,1,0:T(2,128)S(1)} %get-tuple-element.12), channel_id=1, source_target_pairs={{0,2},{2,0},{1,3},{3,1},{4,6},{6,4},{5,7},{7,5},{8,10},{10,8},{9,1... | collective-permute-start | bytes 63656 | tf_op jit(solution)/shard_map/ppermute | solution.py:321
  62.6 3.6 %collective-permute-start.7 = (f32[2,663]{1,0:T(2,128)S(1)}, f32[2,663]{1,0:T(2,128)S(1)}, u32[]{:S(2)}, u32[]{:S(2)}) collective-permute-start(f32[2,663]{1,0:T(2,128)S(1)} %add_add_fusion), channel_id=1, source_target_pairs={{0,4},{4,0},{8,12},{12,8},{1,5},{5,1},{9,13},{13,9},{2,6},{6,2},{1... | collective-permute-start | bytes 15920 | tf_op jit(solution)/shard_map/ppermute | solution.py:321
  66.2 4.8 %collective-permute-start.8 = (f32[2,663]{1,0:T(2,128)S(1)}, f32[2,663]{1,0:T(2,128)S(1)}, u32[]{:S(2)}, u32[]{:S(2)}) collective-permute-start(f32[2,663]{1,0:T(2,128)S(1)} %add.34), channel_id=1, source_target_pairs={{0,12},{12,0},{4,8},{8,4},{1,13},{13,1},{5,9},{9,5},{2,14},{14,2},... | collective-permute-start | bytes 15920 | tf_op jit(solution)/shard_map/ppermute | solution.py:321
  71.1 5.1 %collective-permute-start.9 = (f32[2,663]{1,0:T(2,128)S(1)}, f32[2,663]{1,0:T(2,128)S(1)}, u32[]{:S(2)}, u32[]{:S(2)}) collective-permute-start(f32[2,663]{1,0:T(2,128)S(1)} %add.35), channel_id=1, source_target_pairs={{0,16},{16,0},{1,17},{17,1},{2,18},{18,2},{3,19},{19,3},{4,20},{20... | collective-permute-start | bytes 15920 | tf_op jit(solution)/shard_map/ppermute | solution.py:321

commit v5 on v4

--- a/solution.py
+++ b/solution.py
@@ -143,7 +143,7 @@
 
     def group(g, carry):
         before(g)
-        rolled[...] = pltpu.roll(columns[...], 128 - g * unroll, 1)
+        rolled[...] = pltpu.roll(columns[...], (128 - g * unroll) % 128, 1)
         for j in range(unroll):
             pair = g * unroll + j
             picked = pl.ds(pair, 8, stride=PAIRS)
@@ -170,7 +170,11 @@
         after(g)
         return carry
 
-    lax.fori_loop(0, PAIRS // unroll, group, 0)
+    if slot == 0:
+        lax.fori_loop(0, PAIRS // unroll, group, 0)
+        return
+    for g in range(PAIRS // unroll):
+        group(g, 0)
 
 
 def own_kernel(ranks_ref, ops_ref, table_ref, show_ref, contact_ref, *scratch):
@@ -191,7 +195,6 @@
     values_ref, flop_ref, new_first_ref, new_second_ref = refs[12:16]
     fresh, ready, contact_other, staged_in, staged_out = refs[16:21]
     sums = (show_own, ready, contact_own, contact_other)
-    ready[...] = jnp.zeros_like(ready)
 
     turn_ref, pot_ref, bet_ref, river_ref = inputs[:4]
 
@@ -218,7 +221,8 @@
         fresh[tile, pl.ds(j, 8, stride=RIVERS_HERE), :] = value
 
     def before(g):
-        settle_turn(jnp.maximum(g - 1, 0))
+        if g > 0:
+            settle_turn(g - 1)
 
     def after(g):
         ready[...] = fresh[...]
@@ -251,7 +255,7 @@
 
     def rows_of(ref, c):
         start = c * PAIRS + turn * RIVERS_HERE
-        return ref[pl.ds(pl.multiple_of(start, 8), RIVERS_HERE), :]
+        return ref[pl.ds(start, RIVERS_HERE), :]
 
     def show(c):
         return rows_of(show_own, c) + show_other[c * RIVERS_HERE : (c + 1) * RIVERS_HERE, :]

time: 76.9 us -> 75.4 us (0.980)
  Pallas kernels: 41 us -> 39.6 us
    pallas_call x1, Pallas kernels: 20.5 us -> 19.1 us  [shards(): pl.pallas_call(final_kernel, out_shape=(jax.ShapeDtypeStruct((TURNS_HERE,...]
where the time goes in v5:
time: 75.4 us; the launch traced here: 75.3 us
  Pallas kernels  39.6 us (53%)
  waiting for transfers between devices  17.8 us (24%)
  starting transfers between devices  14.6 us (19%)
  local copies, waits for them, and re-layouts  1.25 us (2%)
  other arithmetic  1.25 us (2%)
  between operations  0.77 us (1%)
    pallas_call x1, Pallas kernels, shards(): pl.pallas_call(final_kernel, out_shape=(jax.ShapeDtypeStruct((TURNS_HERE,...  19.1 us
    pallas_call x1, Pallas kernels, shards(): pl.pallas_call(own_kernel, out_shape=(jax.ShapeDtypeStruct(show_shape, jn...  17.6 us
    ppermute x8, waiting for transfers between devices, exchange(): lax.ppermute(value, axis, [p for a, b in pairs for p in ((a, b), (b, a))])  9.73 us
    ppermute x8, starting transfers between devices, exchange(): lax.ppermute(value, axis, [p for a, b in pairs for p in ((a, b), (b, a))])  9.68 us
    ppermute x1, waiting for transfers between devices, depth_sum(): near = lax.ppermute(value, axes, routes(-1, 1))  5.54 us
    ppermute x1, starting transfers between devices, depth_sum(): far = lax.ppermute(sent, axes, routes(3, -3))  2.99 us
    pallas_call x1, Pallas kernels, shards(): pl.pallas_call(operand_kernel, grid=(TILES // STEP_TILES,), out_shape=jax...  2.97 us
    ppermute x1, waiting for transfers between devices, depth_sum(): far = lax.ppermute(sent, axes, routes(3, -3))  2.52 us
  transfers between devices with their start and end apart: 10, of which 9 were waited for; matrix products, arithmetic and copies ran while one was open for 1% of the time, Pallas kernels for 23%

profile of v5, /device:TPU:2, one launch (start us, length us, event | category | flops | bytes accessed | tf_op | source)
XLA Modules:
  0.0 75.3 jit_solution(16956432507017026911)
XLA Ops:
  0.7 3.0 %shard_map.129.ops_ref = bf16[6,576,128]{2,1,0:T(8,128)(2,1)} custom-call(s32[4,4]{1,0:T(4,128)} %refs_0_.2, s32[4,24]{1,0:T(4,128)} %refs_3_.3, s32[2,2,768]{2,1,0:T(2,128)} %constant.13.clone.refs_0_.refs_1_.refs_2_.refs_4_, s32[2,2,768]{2,1,0:T(2,128)} %constant.13.clone.refs_0_.refs_1_.refs_2_.refs_4_, ...), custom_call_target="tpu_custom_call" | custom-call | flops 4194304 | bytes 4194304 | tf_op jit(solution)/shard_map/pallas_call | solution.py:368
  3.6 2.4 %collective-permute-start = (bf16[6,576,128]{2,1,0:T(8,128)(2,1)}, bf16[6,576,128]{2,1,0:T(8,128)(2,1)S(1)}, u32[]{:S(2)}, u32[]{:S(2)}) collective-permute-start(bf16[6,576,128]{2,1,0:T(8,128)(2,1)} %shard_map.129.ops_ref), channel_id=1, source_target_pairs={{0,1},{1,0},{2,3},{3,2},{4,5},{5,4},{6,7},{7,6},{8,9},{9,8},{10,11... | collective-permute-start | bytes 2654216 | tf_op jit(solution)/shard_map/ppermute | solution.py:325
  6.0 1.2 %copy-done.2 = bf16[6,576,128]{2,1,0:T(8,128)(2,1)S(1)} copy-done((bf16[6,576,128]{2,1,0:T(8,128)(2,1)S(1)}, bf16[6,576,128]{2,1,0:T(8,128)(2,1)}, u32[]{:S(2)}) %copy-start.2) | copy-done | bytes 884760
  7.2 17.6 %shard_map.130 = (f32[6,768,128]{2,1,0:T(8,128)S(1)}, f32[6,576,128]{2,1,0:T(8,128)S(1)}) custom-call(s32[96,1326]{1,0:T(8,128)S(1)} %bitcast.14, bf16[6,576,128]{2,1,0:T(8,128)(2,1)S(1)} %copy-done.2, bf16[2,2,768,768]{3,2,1,0:T(8,128)(2,1)S(1)} %copy-done.9), custom_call_target="tpu_custom_call" | custom-call | flops 25367150592 | bytes 8388608 | tf_op jit(solution)/shard_map/pallas_call | solution.py:390
  24.8 0.5 collective-permute-done.refs_6_
  25.4 19.1 %shard_map.131 = (f32[4,2,663]{2,1,0:T(2,128)S(1)}, f32[2,663]{1,0:T(2,128)S(1)}, f32[4,3,24,663]{3,2,1,0:T(8,128)}, f32[96,4,663]{2,1,0:T(4,128)}) custom-call(s32[4,4]{1,0:T(4,128)S(1)} %copy-done.4, s32[4]{0:T(128)S(1)} %copy-done.8, s32[2,4]{1,0:T(2,128)S(1)} %bitcast.16, s32[4,24]{1,0:T(4,128)S(1)} %copy-done.5, s32[2,2,768]{2,1,0:T(2,128)S(1)} %copy-done.3, ...), custom_call_target="tpu_custom_call" | custom-call | flops 25367150592 | bytes 8388608 | tf_op jit(solution)/shard_map/pallas_call | solution.py:406
  44.5 0.1 collective-permute-start.2
  44.6 1.2 %collective-permute-done.2 = f32[2,663]{1,0:T(2,128)S(1)} collective-permute-done((f32[2,663]{1,0:T(2,128)S(1)}, f32[2,663]{1,0:T(2,128)S(1)}, u32[]{:S(2)}, u32[]{:S(2)}) %collective-permute-start.2) | collective-permute-done | bytes 5336 | tf_op jit(solution)/shard_map/ppermute | solution.py:325
  45.7 1.9 %collective-permute-start.3 = (f32[2,663]{1,0:T(2,128)S(1)}, f32[2,663]{1,0:T(2,128)S(1)}, u32[]{:S(2)}, u32[]{:S(2)}) collective-permute-start(f32[2,663]{1,0:T(2,128)S(1)} %add.29), channel_id=1, source_target_pairs={{224,0},{34,2},{0,32},{66,34},{32,64},{98,66},{64,96},{130,98},{96... | collective-permute-start | bytes 15920 | tf_op jit(solution)/shard_map/ppermute | solution.py:337
  47.6 5.5 %collective-permute-done.3 = f32[2,663]{1,0:T(2,128)S(1)} collective-permute-done((f32[2,663]{1,0:T(2,128)S(1)}, f32[2,663]{1,0:T(2,128)S(1)}, u32[]{:S(2)}, u32[]{:S(2)}) %collective-permute-start.3) | collective-permute-done | bytes 5336 | tf_op jit(solution)/shard_map/ppermute | solution.py:337
  53.2 1.2 %collective-permute-done.4 = f32[2,663]{1,0:T(2,128)S(1)} collective-permute-done((f32[2,663]{1,0:T(2,128)S(1)}, f32[2,663]{1,0:T(2,128)S(1)}, u32[]{:S(2)}, u32[]{:S(2)}) %collective-permute-start.4) | collective-permute-done | bytes 5336 | tf_op jit(solution)/shard_map/ppermute | solution.py:325
  54.4 3.0 %collective-permute-start.5 = (f32[2,663]{1,0:T(2,128)S(1)}, f32[2,663]{1,0:T(2,128)S(1)}, u32[]{:S(2)}, u32[]{:S(2)}) collective-permute-start(f32[2,663]{1,0:T(2,128)S(1)} %get-tuple-element.16), channel_id=1, source_target_pairs={{96,0},{162,2},{128,32},{194,34},{160,64},{226,66},{192,96},{2,98}... | collective-permute-start | bytes 15920 | tf_op jit(solution)/shard_map/ppermute | solution.py:340
  57.4 2.5 %collective-permute-done.5 = f32[2,663]{1,0:T(2,128)S(1)} collective-permute-done((f32[2,663]{1,0:T(2,128)S(1)}, f32[2,663]{1,0:T(2,128)S(1)}, u32[]{:S(2)}, u32[]{:S(2)}) %collective-permute-start.5) | collective-permute-done | bytes 5336 | tf_op jit(solution)/shard_map/ppermute | solution.py:340
  59.9 0.2 collective-permute-start.6
  60.1 0.3 collective-permute-start.1
  60.4 0.7 collective-permute-done.6
  61.1 1.6 %collective-permute-start.7 = (f32[2,663]{1,0:T(2,128)S(1)}, f32[2,663]{1,0:T(2,128)S(1)}, u32[]{:S(2)}, u32[]{:S(2)}) collective-permute-start(f32[2,663]{1,0:T(2,128)S(1)} %add_add_fusion), channel_id=1, source_target_pairs={{0,4},{4,0},{8,12},{12,8},{1,5},{5,1},{9,13},{13,9},{2,6},{6,2},{1... | collective-permute-start | bytes 15920 | tf_op jit(solution)/shard_map/ppermute | solution.py:325
  62.6 2.1 %collective-permute-done.7 = f32[2,663]{1,0:T(2,128)S(1)} collective-permute-done((f32[2,663]{1,0:T(2,128)S(1)}, f32[2,663]{1,0:T(2,128)S(1)}, u32[]{:S(2)}, u32[]{:S(2)}) %collective-permute-start.7) | collective-permute-done | bytes 5336 | tf_op jit(solution)/shard_map/ppermute | solution.py:325
  64.7 3.0 %collective-permute-start.8 = (f32[2,663]{1,0:T(2,128)S(1)}, f32[2,663]{1,0:T(2,128)S(1)}, u32[]{:S(2)}, u32[]{:S(2)}) collective-permute-start(f32[2,663]{1,0:T(2,128)S(1)} %add.34), channel_id=1, source_target_pairs={{0,12},{12,0},{4,8},{8,4},{1,13},{13,1},{5,9},{9,5},{2,14},{14,2},... | collective-permute-start | bytes 15920 | tf_op jit(solution)/shard_map/ppermute | solution.py:325
  67.7 1.8 %collective-permute-done.8 = f32[2,663]{1,0:T(2,128)S(1)} collective-permute-done((f32[2,663]{1,0:T(2,128)S(1)}, f32[2,663]{1,0:T(2,128)S(1)}, u32[]{:S(2)}, u32[]{:S(2)}) %collective-permute-start.8) | collective-permute-done | bytes 5336 | tf_op jit(solution)/shard_map/ppermute | solution.py:325
  69.5 2.1 %collective-permute-start.9 = (f32[2,663]{1,0:T(2,128)S(1)}, f32[2,663]{1,0:T(2,128)S(1)}, u32[]{:S(2)}, u32[]{:S(2)}) collective-permute-start(f32[2,663]{1,0:T(2,128)S(1)} %add.35), channel_id=1, source_target_pairs={{0,16},{16,0},{1,17},{17,1},{2,18},{18,2},{3,19},{19,3},{4,20},{20... | collective-permute-start | bytes 15920 | tf_op jit(solution)/shard_map/ppermute | solution.py:325
  71.7 0.6 add_multiply_fusion
  72.3 2.4 %collective-permute-done.9 = f32[2,663]{1,0:T(2,128)S(1)} collective-permute-done((f32[2,663]{1,0:T(2,128)S(1)}, f32[2,663]{1,0:T(2,128)S(1)}, u32[]{:S(2)}, u32[]{:S(2)}) %collective-permute-start.9) | collective-permute-done | bytes 5336 | tf_op jit(solution)/shard_map/ppermute | solution.py:325
  74.7 0.6 add.36
  (28 shorter events, 0.1 us)
Async XLA Ops:
  0.6 5.4 %copy-start.6 = (s32[4,24,1326]{2,1,0:T(8,128)S(1)}, s32[4,24,1326]{2,1,0:T(8,128)}, u32[]{:S(2)}) copy-start(s32[4,24,1326]{2,1,0:T(8,128)} %param.13) | copy-start | bytes 1527556
  0.6 5.4 %copy-start.9 = (bf16[2,2,768,768]{3,2,1,0:T(8,128)(2,1)S(1)}, bf16[2,2,768,768]{3,2,1,0:T(8,128)(2,1)}, u32[]{:S(2)}) copy-start(bf16[2,2,768,768]{3,2,1,0:T(8,128)(2,1)} %constant.23.table_ref.refs_7_) | copy-start | bytes 14155780
  3.6 21.7 %collective-permute-start = (bf16[6,576,128]{2,1,0:T(8,128)(2,1)}, bf16[6,576,128]{2,1,0:T(8,128)(2,1)S(1)}, u32[]{:S(2)}, u32[]{:S(2)}) collective-permute-start(bf16[6,576,128]{2,1,0:T(8,128)(2,1)} %shard_map.129.ops_ref), channel_id=1, source_target_pairs={{0,1},{1,0},{2,3},{3,2},{4,5},{5,4},{6,7},{7,6},{8,9},{9,8},{10,11... | collective-permute-start | bytes 2654216 | tf_op jit(solution)/shard_map/ppermute | solution.py:325
  6.0 1.2 %copy-start.2 = (bf16[6,576,128]{2,1,0:T(8,128)(2,1)S(1)}, bf16[6,576,128]{2,1,0:T(8,128)(2,1)}, u32[]{:S(2)}) copy-start(bf16[6,576,128]{2,1,0:T(8,128)(2,1)} %shard_map.129.ops_ref) | copy-start | bytes 2654212
  7.2 18.1 %copy-start = (f32[4,24,4,663]{3,2,1,0:T(4,128)S(1)}, f32[4,24,4,663]{3,2,1,0:T(4,128)}, u32[]{:S(2)}) copy-start(f32[4,24,4,663]{3,2,1,0:T(4,128)} %param.17) | copy-start | bytes 3055108
  7.2 18.1 %copy-start.1 = (f32[4,24,3,663]{3,1,2,0:T(8,128)S(1)}, f32[4,24,3,663]{3,1,2,0:T(8,128)}, u32[]{:S(2)}) copy-start(f32[4,24,3,663]{3,1,2,0:T(8,128)} %param.16) | copy-start | bytes 2291332
  7.2 18.1 %copy-start.3 = (s32[2,2,768]{2,1,0:T(2,128)S(1)}, s32[2,2,768]{2,1,0:T(2,128)}, u32[]{:S(2)}) copy-start(s32[2,2,768]{2,1,0:T(2,128)} %constant.13.clone.refs_0_.refs_1_.refs_2_.refs_4_) | copy-start | bytes 36868
  7.2 18.1 %copy-start.4 = (s32[4,4]{1,0:T(4,128)S(1)}, s32[4,4]{1,0:T(4,128)}, u32[]{:S(2)}) copy-start(s32[4,4]{1,0:T(4,128)} %refs_0_.2) | copy-start | bytes 196
  7.2 18.1 %copy-start.5 = (s32[4,24]{1,0:T(4,128)S(1)}, s32[4,24]{1,0:T(4,128)}, u32[]{:S(2)}) copy-start(s32[4,24]{1,0:T(4,128)} %refs_3_.3) | copy-start | bytes 1156
  7.2 18.1 %copy-start.7 = (s32[4,2]{0,1:T(2,128)S(1)}, s32[4,2]{0,1:T(2,128)}, u32[]{:S(2)}) copy-start(s32[4,2]{0,1:T(2,128)} %param.15) | copy-start | bytes 100
  7.2 18.1 %copy-start.8 = (s32[4]{0:T(128)S(1)}, s32[4]{0:T(128)}, u32[]{:S(2)}) copy-start(s32[4]{0:T(128)} %refs_1_.2) | copy-start | bytes 52
  7.2 18.1 %copy-start.10 = (bf16[2,2,768,768]{3,2,1,0:T(8,128)(2,1)S(1)}, bf16[2,2,768,768]{3,2,1,0:T(8,128)(2,1)}, u32[]{:S(2)}) copy-start(bf16[2,2,768,768]{3,2,1,0:T(8,128)(2,1)} %constant.23.table_ref.refs_7_) | copy-start | bytes 14155780
  44.5 1.3 %collective-permute-start.2 = (f32[2,663]{1,0:T(2,128)S(1)}, f32[2,663]{1,0:T(2,128)S(1)}, u32[]{:S(2)}, u32[]{:S(2)}) collective-permute-start(f32[2,663]{1,0:T(2,128)S(1)} %get-tuple-element.13), channel_id=1, source_target_pairs={{0,2},{2,0},{1,3},{3,1},{4,6},{6,4},{5,7},{7,5},{8,10},{10,8},{9,1... | collective-permute-start | bytes 15920 | tf_op jit(solution)/shard_map/ppermute | solution.py:325
  45.7 7.5 %collective-permute-start.3 = (f32[2,663]{1,0:T(2,128)S(1)}, f32[2,663]{1,0:T(2,128)S(1)}, u32[]{:S(2)}, u32[]{:S(2)}) collective-permute-start(f32[2,663]{1,0:T(2,128)S(1)} %add.29), channel_id=1, source_target_pairs={{224,0},{34,2},{0,32},{66,34},{32,64},{98,66},{64,96},{130,98},{96... | collective-permute-start | bytes 15920 | tf_op jit(solution)/shard_map/ppermute | solution.py:337
  53.2 1.2 %collective-permute-start.4 = (f32[2,663]{1,0:T(2,128)S(1)}, f32[2,663]{1,0:T(2,128)S(1)}, u32[]{:S(2)}, u32[]{:S(2)}) collective-permute-start(f32[2,663]{1,0:T(2,128)S(1)} %collective-permute-done.3), channel_id=1, source_target_pairs={{0,2},{2,0},{1,3},{3,1},{4,6},{6,4},{5,7},{7,5},{8,10},{10,8},{9,1... | collective-permute-start | bytes 15920 | tf_op jit(solution)/shard_map/ppermute | solution.py:325
  54.4 5.5 %collective-permute-start.5 = (f32[2,663]{1,0:T(2,128)S(1)}, f32[2,663]{1,0:T(2,128)S(1)}, u32[]{:S(2)}, u32[]{:S(2)}) collective-permute-start(f32[2,663]{1,0:T(2,128)S(1)} %get-tuple-element.16), channel_id=1, source_target_pairs={{96,0},{162,2},{128,32},{194,34},{160,64},{226,66},{192,96},{2,98}... | collective-permute-start | bytes 15920 | tf_op jit(solution)/shard_map/ppermute | solution.py:340
  59.9 1.2 %collective-permute-start.6 = (f32[2,663]{1,0:T(2,128)S(1)}, f32[2,663]{1,0:T(2,128)S(1)}, u32[]{:S(2)}, u32[]{:S(2)}) collective-permute-start(f32[2,663]{1,0:T(2,128)S(1)} %collective-permute-done.5), channel_id=1, source_target_pairs={{0,2},{2,0},{1,3},{3,1},{4,6},{6,4},{5,7},{7,5},{8,10},{10,8},{9,1... | collective-permute-start | bytes 15920 | tf_op jit(solution)/shard_map/ppermute | solution.py:325
  60.1 11.6 %collective-permute-start.1 = (f32[4,2,663]{2,1,0:T(2,128)S(1)}, f32[4,2,663]{2,1,0:T(2,128)S(1)}, u32[]{:S(2)}, u32[]{:S(2)}) collective-permute-start(f32[4,2,663]{2,1,0:T(2,128)S(1)} %get-tuple-element.12), channel_id=1, source_target_pairs={{0,2},{2,0},{1,3},{3,1},{4,6},{6,4},{5,7},{7,5},{8,10},{10,8},{9,1... | collective-permute-start | bytes 63656 | tf_op jit(solution)/shard_map/ppermute | solution.py:325
  61.1 3.6 %collective-permute-start.7 = (f32[2,663]{1,0:T(2,128)S(1)}, f32[2,663]{1,0:T(2,128)S(1)}, u32[]{:S(2)}, u32[]{:S(2)}) collective-permute-start(f32[2,663]{1,0:T(2,128)S(1)} %add_add_fusion), channel_id=1, source_target_pairs={{0,4},{4,0},{8,12},{12,8},{1,5},{5,1},{9,13},{13,9},{2,6},{6,2},{1... | collective-permute-start | bytes 15920 | tf_op jit(solution)/shard_map/ppermute | solution.py:325
  64.7 4.8 %collective-permute-start.8 = (f32[2,663]{1,0:T(2,128)S(1)}, f32[2,663]{1,0:T(2,128)S(1)}, u32[]{:S(2)}, u32[]{:S(2)}) collective-permute-start(f32[2,663]{1,0:T(2,128)S(1)} %add.34), channel_id=1, source_target_pairs={{0,12},{12,0},{4,8},{8,4},{1,13},{13,1},{5,9},{9,5},{2,14},{14,2},... | collective-permute-start | bytes 15920 | tf_op jit(solution)/shard_map/ppermute | solution.py:325
  69.5 5.1 %collective-permute-start.9 = (f32[2,663]{1,0:T(2,128)S(1)}, f32[2,663]{1,0:T(2,128)S(1)}, u32[]{:S(2)}, u32[]{:S(2)}) collective-permute-start(f32[2,663]{1,0:T(2,128)S(1)} %add.35), channel_id=1, source_target_pairs={{0,16},{16,0},{1,17},{17,1},{2,18},{18,2},{3,19},{19,3},{4,20},{20... | collective-permute-start | bytes 15920 | tf_op jit(solution)/shard_map/ppermute | solution.py:325
